TPU v7x, 256 devices: a whole 4x4x8 slice. The times are simulated.
256 devices in a mesh: cluster: 16 (over z, core), group: 16 (over y, x).
Axes of the slice: x: 4, y: 4, z: 8, core: 2. Of those that a mesh axis runs over, the one named last changes fastest.
Arguments:
- loads: float32 [256, 8, 128, 256], P(('cluster', 'group')), parts along dimension 0, may hold values from -6 to 6
- multipliers: float32 [131072, 256], P(('cluster', 'group')), parts along dimension 0, may hold values from -6 to 6
- gluing: int32 [131072], P(('cluster', 'group')), parts along dimension 0, may hold values from 0 to 16383
- signs: int32 [131072], P(('cluster', 'group')), parts along dimension 0, may hold values 0 or 1
- parents: int32 [256, 7], P('cluster'), parts along dimension 0, may hold values from 0 to 15
- inverses: float32 [256, 8, 128, 128], P(('cluster', 'group')), parts along dimension 0
- to_parent: float32 [256, 7, 128, 128], P(('cluster', 'group')), parts along dimension 0, may hold values from -0.25 to 0.25
- grandparent_factor: float32 [256, 6, 128, 128], P(('cluster', 'group')), parts along dimension 0, may hold values from -0.25 to 0.25
Outputs:
- solved: float32 [256, 8, 128, 256], P(('cluster', 'group')), parts along dimension 0
There are 16 independent parts, one for each index of `cluster`. A program takes and returns all parts, laid end to end along the dimension named above; each array names one. Nothing has to cross between parts.
Inputs may be any that keep to these rules, and one draw needn't show every extreme that they name: gluing[m] = (n * 8 + l) * 128 + i names row i of supernode n on level l; several multipliers may glue one unknown. parents[n, l] is the supernode on level l + 1 into which supernode n of level l is eliminated.
All inputs are finite; a program needn't handle non-finite values. No bound on the sum of `signs` on one device may be relied on, other than what follows from the above.
Results may differ from a plain program's by a relative error of at most 0.0001.
Values sent between devices are 32-bit elements; how exact they have to be, the bound alone decides.
A program may use at most 64 MiB of HBM per device.

v0:
```python
import jax
import jax.numpy as jnp
from jax import lax
from jax.sharding import PartitionSpec as P


def body(loads, multipliers, gluing, signs, parents, inverses, to_parent, grandparent_factor):
    me = lax.axis_index("group")
    tree_depths = loads.shape[1]
    rows = loads.shape[2]
    span = tree_depths * rows
    coeff = (2 * signs - 1).astype(jnp.float32)
    target = lax.iota(jnp.int32, lax.axis_size("group") * span)
    table = jnp.where(target[:, None] == gluing[None, :], coeff[None, :], 0.0)
    glued = lax.psum_scatter(
        jnp.dot(
            table, multipliers, precision=lax.Precision.HIGHEST, preferred_element_type=jnp.float32
        ),
        "group",
        scatter_dimension=0,
        tiled=True,
    )
    awaiting_contribution = [
        loads[0, level] - glued[level * rows : (level + 1) * rows] for level in range(tree_depths)
    ]
    node_count = parents.shape[0]
    solved = []
    for level in range(tree_depths):
        unknown_estimate = jnp.dot(
            inverses[0, level],
            awaiting_contribution[level],
            precision=lax.Precision.HIGHEST,
            preferred_element_type=jnp.float32,
        )
        solved.append(unknown_estimate)
        if level + 1 < tree_depths:
            first = parents[:, level]
            if level + 2 < tree_depths:
                match = first[:, None] == lax.iota(jnp.int32, node_count)[None, :]
                second_term = jnp.sum(jnp.where(match, parents[None, :, level + 1], 0), axis=1)
                targets = jnp.stack([first, second_term], axis=1)
                panel_sequence = jnp.stack([to_parent[0, level], grandparent_factor[0, level]])
            else:
                targets = first[:, None]
                panel_sequence = to_parent[0, level][None]
            update_terms = jnp.einsum(
                "xdf,fh->xdh", panel_sequence, unknown_estimate, precision=lax.Precision.HIGHEST
            )[None]
            weight = (targets == me).astype(jnp.float32)
            moved = jnp.einsum(
                "km,kmbr->mbr",
                weight,
                lax.all_gather(update_terms, "group", axis=0, tiled=True),
                precision=lax.Precision.HIGHEST,
            )
            awaiting_contribution[level + 1] = awaiting_contribution[level + 1] - moved[0]
            if level + 2 < tree_depths:
                awaiting_contribution[level + 2] = awaiting_contribution[level + 2] - moved[1]
    return jnp.stack(solved)[None]


def solution(mesh):
    return jax.shard_map(
        body,
        mesh=mesh,
        in_specs=(
            P(("cluster", "group"), None, None, None),
            P(("cluster", "group"), None),
            P(("cluster", "group")),
            P(("cluster", "group")),
            P("cluster", None),
            P(("cluster", "group"), None, None, None),
            P(("cluster", "group"), None, None, None),
            P(("cluster", "group"), None, None, None),
        ),
        out_specs=P(("cluster", "group"), None, None, None),
        check_vma=False,
    )
```

profile of v0, /device:TPU:96, one launch (start us, length us, event | category | flops | bytes accessed | tf_op | source)
XLA Modules:
  0.0 614.1 jit_solution(14356291022115446529)
XLA Ops:
  6.5 0.0 copy-start
  6.5 0.0 reduce-scatter.2.cloned.1.call-start
  6.5 0.7 add_convert_fusion
  7.3 0.3 copy-done
  7.6 30.6 %fusion = f32[16384,256]{1,0:T(8,128)} fusion(f32[512,256]{1,0:T(8,128)S(1)} %copy-done, f32[512]{0:T(512)S(1)} %add_convert_fusion, s32[512]{0:T(512)} %param.10), kind=kOutput, calls=%fused_computation | convolution fusion | flops 25786580992 | bytes 17305600 | tf_op jit(solution)/shard_map/dot_general | solution.py:16
  38.2 0.0 copy-start.2
  38.2 0.0 reduce-scatter.2.cloned.1.call-update
  38.2 0.0 all-gather.15.cloned.1.call-start
  38.3 0.9 copy-done.2
  39.2 0.1 copy-done.3
  39.3 0.8 slice_bitcast_fusion.12
  40.1 115.8 %reduce-scatter.2.cloned.1.call-done = f32[1024,256]{1,0:T(8,128)} async-done(((f32[16384,256]{1,0:T(8,128)}), f32[1024,256]{1,0:T(8,128)}) %reduce-scatter.2.cloned.1.call-update) | async-done | bytes 1048592 | tf_op jit(solution)/shard_map/reduce_scatter | solution.py:15
  155.9 0.0 copy-done.1
  155.9 1.3 bitcast_dynamic-update-slice_fusion.6
  157.2 1.1 fusion.50
  158.3 0.0 all-gather.15.cloned.1.call-update
  158.3 0.5 all-gather.17.cloned.1.call-start
  158.8 0.0 copy-done.4
  158.8 0.6 fusion.133
  159.4 0.8 select_reduce_fusion
  160.3 54.4 %all-gather.15.cloned.1.call-done = f32[32,128,256]{2,1,0:T(8,128)} async-done(((f32[2,128,256]{2,1,0:T(8,128)}), f32[32,128,256]{2,1,0:T(8,128)}) %all-gather.15.cloned.1.call-update) | async-done | bytes 4194320 | tf_op jit(solution)/shard_map/all_gather | solution.py:53
  214.7 5.8 fusion.15
  220.5 1.3 bitcast_dynamic-update-slice_fusion.5
  221.8 1.1 fusion.54
  222.9 0.0 all-gather.17.cloned.1.call-update
  222.9 0.0 all-gather.19.cloned.1.call-start
  223.0 56.4 %all-gather.17.cloned.1.call-done = f32[32,128,256]{2,1,0:T(8,128)} async-done(((f32[2,128,256]{2,1,0:T(8,128)}), f32[32,128,256]{2,1,0:T(8,128)}) %all-gather.17.cloned.1.call-update) | async-done | bytes 4194320 | tf_op jit(solution)/shard_map/all_gather | solution.py:53
  279.4 5.8 fusion.13
  285.2 1.3 bitcast_dynamic-update-slice_fusion.4
  286.6 2.0 fusion.58
  288.5 0.0 all-gather.19.cloned.1.call-update
  288.5 0.2 all-gather.21.cloned.1.call-start
  288.8 0.7 compare_bitcast_fusion.3
  289.5 55.5 %all-gather.19.cloned.1.call-done = f32[32,128,256]{2,1,0:T(8,128)} async-done(((f32[2,128,256]{2,1,0:T(8,128)}), f32[32,128,256]{2,1,0:T(8,128)}) %all-gather.19.cloned.1.call-update) | async-done | bytes 4194320 | tf_op jit(solution)/shard_map/all_gather | solution.py:53
  345.0 5.8 fusion.11
  350.9 1.3 bitcast_dynamic-update-slice_fusion.3
  352.2 1.1 fusion.62
  353.2 0.0 all-gather.21.cloned.1.call-update
  353.3 0.0 all-gather.23.cloned.1.call-start
  353.3 0.7 compare_bitcast_fusion.2
  354.0 55.7 %all-gather.21.cloned.1.call-done = f32[32,128,256]{2,1,0:T(8,128)} async-done(((f32[2,128,256]{2,1,0:T(8,128)}), f32[32,128,256]{2,1,0:T(8,128)}) %all-gather.21.cloned.1.call-update) | async-done | bytes 4194320 | tf_op jit(solution)/shard_map/all_gather | solution.py:53
  409.7 5.8 fusion.9
  415.6 1.3 bitcast_dynamic-update-slice_fusion.2
  416.9 2.0 fusion.66
  418.8 0.0 all-gather.23.cloned.1.call-update
  418.9 0.3 all-gather.25.cloned.1.call-start
  419.1 0.6 compare_bitcast_fusion.1
  419.7 55.6 %all-gather.23.cloned.1.call-done = f32[32,128,256]{2,1,0:T(8,128)} async-done(((f32[2,128,256]{2,1,0:T(8,128)}), f32[32,128,256]{2,1,0:T(8,128)}) %all-gather.23.cloned.1.call-update) | async-done | bytes 4194320 | tf_op jit(solution)/shard_map/all_gather | solution.py:53
  475.3 5.8 fusion.7
  481.2 1.3 bitcast_dynamic-update-slice_fusion.1
  482.5 1.1 fusion.70
  483.6 0.0 all-gather.25.cloned.1.call-update
  483.6 0.0 all-gather.27.cloned.1.call-start
  483.7 56.4 %all-gather.25.cloned.1.call-done = f32[32,128,256]{2,1,0:T(8,128)} async-done(((f32[2,128,256]{2,1,0:T(8,128)}), f32[32,128,256]{2,1,0:T(8,128)}) %all-gather.25.cloned.1.call-update) | async-done | bytes 4194320 | tf_op jit(solution)/shard_map/all_gather | solution.py:53
  540.0 5.8 fusion.5
  545.9 1.3 bitcast_dynamic-update-slice_fusion
  547.2 1.8 convolution_bitcast_fusion.1
  549.0 0.0 all-gather.27.cloned.1.call-update
  549.0 52.6 %all-gather.27.cloned.1.call-done = f32[2048,256]{0,1:T(8,128)} async-done(((f32[128,256]{0,1:T(8,128)}), f32[2048,256]{0,1:T(8,128)}) %all-gather.27.cloned.1.call-update) | async-done | bytes 2097168 | tf_op jit(solution)/shard_map/all_gather | solution.py:53
  601.6 2.0 copy.31
  603.5 0.8 fusion.121
  604.3 0.1 copy.30
  604.4 1.3 fusion.17
  605.8 1.3 copy.11
  (12 shorter events, 0.2 us)
Async XLA Ops:
  6.5 1.1 copy-start
  6.5 149.4 %reduce-scatter.2.cloned.1.call-start = ((), (), s32[]{:S(2)}) async-start(), calls=%async_computation.1 | async-start | bytes 17825792 | tf_op jit(solution)/shard_map/reduce_scatter | solution.py:15
  38.2 1.0 copy-start.2
  38.2 1.1 copy-start.3
  38.2 117.7 %copy-start.1 = (f32[1,8,128,256]{3,2,1,0:T(8,128)S(1)}, f32[1,8,128,256]{3,2,1,0:T(8,128)}, u32[]{:S(2)}) copy-start(f32[1,8,128,256]{3,2,1,0:T(8,128)} %param.8) | copy-start | bytes 3145732
  38.2 120.6 %copy-start.4 = (s32[16,7]{0,1:T(8,128)S(1)}, s32[16,7]{0,1:T(8,128)}, u32[]{:S(2)}) copy-start(s32[16,7]{0,1:T(8,128)} %param.12) | copy-start | bytes 1348
  38.2 176.4 %all-gather.15.cloned.1.call-start = ((), (), s32[]{:S(2)}) async-start(), calls=%async_computation.2 | async-start | bytes 4456448 | tf_op jit(solution)/shard_map/all_gather | solution.py:53
  158.3 121.1 %all-gather.17.cloned.1.call-start = ((), (), s32[]{:S(2)}) async-start(), calls=%async_computation.3 | async-start | bytes 4456448 | tf_op jit(solution)/shard_map/all_gather | solution.py:53
  222.9 122.0 %all-gather.19.cloned.1.call-start = ((), (), s32[]{:S(2)}) async-start(), calls=%async_computation.4 | async-start | bytes 4456448 | tf_op jit(solution)/shard_map/all_gather | solution.py:53
  288.5 121.2 %all-gather.21.cloned.1.call-start = ((), (), s32[]{:S(2)}) async-start(), calls=%async_computation.5 | async-start | bytes 4456448 | tf_op jit(solution)/shard_map/all_gather | solution.py:53
  353.3 122.0 %all-gather.23.cloned.1.call-start = ((), (), s32[]{:S(2)}) async-start(), calls=%async_computation.6 | async-start | bytes 4456448 | tf_op jit(solution)/shard_map/all_gather | solution.py:53
  418.9 121.2 %all-gather.25.cloned.1.call-start = ((), (), s32[]{:S(2)}) async-start(), calls=%async_computation.7 | async-start | bytes 4456448 | tf_op jit(solution)/shard_map/all_gather | solution.py:53
  483.6 118.0 %all-gather.27.cloned.1.call-start = ((), (), s32[]{:S(2)}) async-start(), calls=%async_computation.8 | async-start | bytes 2228224 | tf_op jit(solution)/shard_map/all_gather | solution.py:53
Sparse Core Ops, SparseCore 0:
  38.4 117.4 reduce-scatter.1
  158.4 56.1 all-gather.14
  223.1 56.2 all-gather.16
  288.7 56.2 all-gather.18
  353.4 56.2 all-gather.20
  419.0 56.2 all-gather.22
  483.7 56.2 all-gather.24
  549.1 52.3 all-gather.26
where the time goes:
time: 622 us; the launch traced here: 614 us
  waiting for transfers between devices  502 us (81%)
  matrix products  86.8 us (14%)
  between operations  13.9 us (2%)
    all_gather x7, waiting for transfers between devices, body(): lax.all_gather(update_terms, 'group', axis=0, tiled=True)  386 us
    reduce_scatter x1, waiting for transfers between devices, body(): lax.psum_scatter(jnp.dot(table, multipliers, precision=lax.Precision.HIGH...  116 us
    dot_general x7, matrix products, body(): jnp.einsum('km,kmbr->mbr', weight, lax.all_gather(update_terms, 'group',...  35.8 us
    dot_general x1, matrix products, body(): jnp.dot(table, multipliers, precision=lax.Precision.HIGHEST, preferred_el...  30.6 us
  transfers between devices with their start and end apart: 8, of which 8 were waited for; matrix products, arithmetic and copies ran while one was open for 1% of the time, Pallas kernels for 0%

commit v1 on v0

--- a/solution.py
+++ b/solution.py
@@ -1,10 +1,296 @@
 import jax
 import jax.numpy as jnp
 from jax import lax
+from jax.experimental import pallas as pl
+from jax.experimental.pallas import tpu as pltpu
 from jax.sharding import PartitionSpec as P
 
-
-def body(loads, multipliers, gluing, signs, parents, inverses, to_parent, grandparent_factor):
+CHUNKS = 4
+SLOTS = 16
+HEAD = 8
+
+
+def split(x):
+    high = x.astype(jnp.bfloat16)
+    return high, (x - high.astype(jnp.float32)).astype(jnp.bfloat16)
+
+
+def mm(a, b):
+    return jnp.dot(a, b, preferred_element_type=jnp.float32)
+
+
+def product(matrix, x):
+    high, low = split(x)
+    return mm(matrix[0], high) + (mm(matrix[0], low) + mm(matrix[1], high))
+
+
+def kernel(
+    loads, multipliers, gluing, signs, parents, inverses, to_parent, grandparent,
+    out, flag,
+    bucket, received, rows_high, rows_low, pending, parent_map,
+    inv_h, inv_l, one_h, one_l, two_h, two_l,
+    one_out, one_in, two_out, two_in, sum_out, sum_in, carried,
+    pack_send, pack_recv, one_send, one_recv, two_send, two_recv, sum_send, sum_recv,
+):
+    nodes = parents.shape[0]
+    levels, rows, columns = loads.shape[1:]
+    count = multipliers.shape[0]
+    me = lax.axis_index("group")
+    others = nodes - 1
+
+    def peer(k):
+        return lax.rem(me + k, nodes)
+
+    barrier = pltpu.get_barrier_semaphore()
+
+    @pl.loop(1, nodes)
+    def _(k):
+        pl.semaphore_signal(barrier, inc=1, device_id={"group": peer(k)}, device_id_type=pl.DeviceIdType.MESH)
+
+    dof = jnp.concatenate([gluing[i : i + 1, :] for i in range(gluing.shape[0])], axis=1)
+    sign = jnp.concatenate([signs[i : i + 1, :] for i in range(signs.shape[0])], axis=1)
+    coeff = (2 * sign - 1).astype(jnp.float32)
+    span = levels * rows
+    node = lax.div(dof, span)
+    row = lax.rem(dof, span)
+    order = lax.broadcasted_iota(jnp.int32, (1, count), 1)
+    key = (dof * count + order).astype(jnp.float32)
+    start = (node * (span * count)).astype(jnp.float32)
+    rank = jnp.zeros((1, count), jnp.float32)
+    for i in range(count // 128):
+        lanes = jnp.broadcast_to(key[:, i * 128 : (i + 1) * 128], (128, 128))
+        down = jnp.transpose(lanes)
+        down = jnp.concatenate([down] * (count // 128), axis=1)
+        before = (down < key) & (down >= start)
+        rank = rank + jnp.sum(jnp.where(before, 1.0, 0.0), axis=0, keepdims=True)
+    rank = rank.astype(jnp.int32)
+    fits = rank < CHUNKS * SLOTS
+    chunk = lax.div(rank, SLOTS)
+    slot = lax.rem(rank, SLOTS)
+    overflow = jnp.max(jnp.where(fits, 0.0, 1.0))
+
+    place = jnp.where(fits, node * HEAD + chunk, -1)
+    owner_rows = lax.broadcasted_iota(jnp.int32, (nodes * HEAD, count), 0) == place
+    low_part = jnp.where(owner_rows, lax.rem(row, rows).astype(jnp.float32), 0.0).astype(jnp.bfloat16)
+    high_part = jnp.where(owner_rows, (lax.div(row, rows) * rows).astype(jnp.float32), 0.0).astype(jnp.bfloat16)
+    lane_of = lax.broadcasted_iota(jnp.int32, (nodes * SLOTS, count), 0) == SLOTS * me + slot
+    lane_of = jnp.where(lane_of, 1.0, 0.0).astype(jnp.bfloat16)
+    contract = (((1,), (1,)), ((), ()))
+    header = lax.dot_general(low_part, lane_of, contract, preferred_element_type=jnp.float32)
+    header = header + lax.dot_general(high_part, lane_of, contract, preferred_element_type=jnp.float32)
+    last = lax.rem(lax.broadcasted_iota(jnp.int32, header.shape, 0), HEAD) == HEAD - 1
+    header = jnp.where(last, overflow, header)
+    bucket[:, 0:HEAD, :] = header.reshape(nodes, HEAD, columns)
+
+    target = jnp.where(fits, chunk * (nodes * SLOTS) + node * SLOTS + slot, -1)
+    m_high, m_low = split(multipliers[...])
+    for j in range(CHUNKS):
+        index = lax.broadcasted_iota(jnp.int32, (nodes * SLOTS, count), 0) + j * nodes * SLOTS
+        table = jnp.where(index == target, coeff, 0.0).astype(jnp.bfloat16)
+        packed = mm(table, m_high) + mm(table, m_low)
+        first = HEAD + j * SLOTS
+        bucket[:, first : first + SLOTS, :] = packed.reshape(nodes, SLOTS, columns)
+
+    pl.semaphore_wait(barrier, others)
+
+    def copy(source, target, send, recv, k):
+        return pltpu.make_async_remote_copy(
+            src_ref=source,
+            dst_ref=target,
+            send_sem=send,
+            recv_sem=recv,
+            device_id={"group": peer(k)},
+            device_id_type=pl.DeviceIdType.MESH,
+        )
+
+    @pl.loop(1, nodes)
+    def _(k):
+        copy(bucket.at[peer(k)], received.at[me], pack_send.at[0], pack_recv.at[0], k).start()
+
+    received[me] = bucket[me]
+
+    @pl.loop(0, levels)
+    def _(l):
+        inv_h[l], inv_l[l] = split(inverses[0, l])
+
+    @pl.loop(0, levels - 1)
+    def _(l):
+        one_h[l], one_l[l] = split(to_parent[0, l])
+
+    @pl.loop(0, levels - 2)
+    def _(l):
+        two_h[l], two_l[l] = split(grandparent[0, l])
+
+    chunk_rows = rows // nodes
+    spread = lax.broadcasted_iota(jnp.int32, (nodes, rows), 1)
+    spread = lax.div(spread, chunk_rows) == lax.broadcasted_iota(jnp.int32, (nodes, rows), 0)
+    spread = jnp.where(spread, 1.0, 0.0).astype(jnp.bfloat16)
+    across = lax.dot_general(
+        parents[...].astype(jnp.float32).astype(jnp.bfloat16),
+        spread,
+        (((0,), (0,)), ((), ())),
+        preferred_element_type=jnp.float32,
+    )
+    down_rows = lax.broadcasted_iota(jnp.int32, (rows, rows), 0)
+    same = lax.rem(down_rows, chunk_rows) == lax.rem(
+        lax.broadcasted_iota(jnp.int32, (rows, rows), 1), chunk_rows
+    )
+    down_node = lax.div(down_rows, chunk_rows)
+    for l in range(levels - 1):
+        hit = same & (down_node == across[l : l + 1, :].astype(jnp.int32))
+        parent_map[l] = jnp.where(hit, 1.0, 0.0).astype(jnp.bfloat16)
+    carried[...] = jnp.zeros_like(carried)
+    sum_in[0] = jnp.zeros_like(sum_in[0])
+
+    copy(bucket.at[pl.ds(0, others)], received.at[pl.ds(0, others)], pack_send.at[0], pack_recv.at[0], 1).wait_recv()
+
+    head = received[0, 0:HEAD, :]
+    for i in range(1, nodes):
+        head = head + received[i, 0:HEAD, :]
+    flag[...] = head[:, 0:128]
+    width = nodes * SLOTS
+    for j in range(CHUNKS):
+        first = HEAD + j * SLOTS
+        high, low = split(received[:, first : first + SLOTS, :].reshape(width, columns))
+        rows_high[j * width : (j + 1) * width] = high
+        rows_low[j * width : (j + 1) * width] = low
+    wanted = jnp.concatenate([head[j : j + 1, :] for j in range(CHUNKS)], axis=1).astype(jnp.int32)
+
+    @pl.loop(0, levels)
+    def _(l):
+        table = lax.broadcasted_iota(jnp.int32, (rows, CHUNKS * width), 0) + l * rows == wanted
+        table = jnp.where(table, 1.0, 0.0).astype(jnp.bfloat16)
+        pending[l] = loads[0, l] - (mm(table, rows_high[...]) + mm(table, rows_low[...]))
+
+    def send(l, source, target, send_sem, recv_sem):
+        @pl.loop(1, nodes)
+        def _(k):
+            copy(source.at[l, peer(k)], target.at[l, me], send_sem.at[l], recv_sem.at[l], k).start()
+
+        target[l, me] = source[l, me]
+
+    def arrived(l, source, target, send_sem, recv_sem):
+        copy(
+            source.at[l, pl.ds(0, others)], target.at[l, pl.ds(0, others)], send_sem.at[l], recv_sem.at[l], 1
+        ).wait_recv()
+
+    def sent(l, source, target, send_sem, recv_sem):
+        copy(
+            source.at[l, pl.ds(0, others)], target.at[l, pl.ds(0, others)], send_sem.at[l], recv_sem.at[l], 1
+        ).wait_send()
+
+    one = (one_out, one_in, one_send, one_recv)
+    two = (two_out, two_in, two_send, two_recv)
+    total = (sum_out, sum_in, sum_send, sum_recv)
+    blocks = (nodes, chunk_rows, columns)
+
+    def solve(l):
+        x = pending[l] - sum_in[l].reshape(rows, columns)
+        x = product((inv_h[l], inv_l[l]), x)
+        out[0, l] = x
+        return x
+
+    @pl.loop(0, levels - 1)
+    def _(l):
+        x = solve(l)
+        one_out[l] = product((one_h[l], one_l[l]), x).reshape(blocks)
+        send(l, *one)
+
+        @pl.when(l < levels - 2)
+        def _():
+            two_out[l] = product((two_h[l], two_l[l]), x).reshape(blocks)
+            send(l, *two)
+
+        arrived(l, *one)
+        high, low = split(one_in[l].reshape(rows, columns) + carried[...])
+        sum_out[l + 1] = (mm(parent_map[l], high) + mm(parent_map[l], low)).reshape(blocks)
+        send(l + 1, *total)
+
+        @pl.when(l < levels - 2)
+        def _():
+            arrived(l, *two)
+            high, low = split(two_in[l].reshape(rows, columns))
+            carried[...] = mm(parent_map[l], high) + mm(parent_map[l], low)
+
+        arrived(l + 1, *total)
+
+    solve(levels - 1)
+
+    copy(bucket.at[pl.ds(0, others)], received.at[pl.ds(0, others)], pack_send.at[0], pack_recv.at[0], 1).wait_send()
+
+    @pl.loop(0, levels - 1)
+    def _(l):
+        sent(l, *one)
+        sent(l + 1, *total)
+
+    @pl.loop(0, levels - 2)
+    def _(l):
+        sent(l, *two)
+
+
+def direct(loads, multipliers, gluing, signs, parents, inverses, to_parent, grandparent_factor):
+    nodes = parents.shape[0]
+    _, levels, rows, columns = loads.shape
+    count = multipliers.shape[0]
+    f32, bf16 = jnp.float32, jnp.bfloat16
+    room = HEAD + CHUNKS * SLOTS
+    blocks = (nodes, rows // nodes, columns)
+    square = (rows, rows)
+    dma = pltpu.SemaphoreType.DMA
+    vmem = pl.BlockSpec(memory_space=pltpu.VMEM)
+    return pl.pallas_call(
+        kernel,
+        out_shape=(
+            jax.ShapeDtypeStruct(loads.shape, f32),
+            jax.ShapeDtypeStruct((HEAD, 128), f32),
+        ),
+        in_specs=[vmem] * 8,
+        out_specs=(vmem, vmem),
+        scratch_shapes=[
+            pltpu.VMEM((nodes, room, columns), f32),
+            pltpu.VMEM((nodes, room, columns), f32),
+            pltpu.VMEM((nodes * CHUNKS * SLOTS, columns), bf16),
+            pltpu.VMEM((nodes * CHUNKS * SLOTS, columns), bf16),
+            pltpu.VMEM((levels, rows, columns), f32),
+            pltpu.VMEM((levels - 1, *square), bf16),
+            pltpu.VMEM((levels, *square), bf16),
+            pltpu.VMEM((levels, *square), bf16),
+            pltpu.VMEM((levels - 1, *square), bf16),
+            pltpu.VMEM((levels - 1, *square), bf16),
+            pltpu.VMEM((levels - 2, *square), bf16),
+            pltpu.VMEM((levels - 2, *square), bf16),
+            pltpu.VMEM((levels - 1, *blocks), f32),
+            pltpu.VMEM((levels - 1, *blocks), f32),
+            pltpu.VMEM((levels - 2, *blocks), f32),
+            pltpu.VMEM((levels - 2, *blocks), f32),
+            pltpu.VMEM((levels, *blocks), f32),
+            pltpu.VMEM((levels, *blocks), f32),
+            pltpu.VMEM((rows, columns), f32),
+            dma((1,)),
+            dma((1,)),
+            dma((levels - 1,)),
+            dma((levels - 1,)),
+            dma((levels - 2,)),
+            dma((levels - 2,)),
+            dma((levels,)),
+            dma((levels,)),
+        ],
+        compiler_params=pltpu.CompilerParams(
+            collective_id=0, has_side_effects=True, vmem_limit_bytes=48 * 1024 * 1024
+        ),
+    )(
+        loads,
+        multipliers,
+        gluing.reshape(count // 128, 128),
+        signs.reshape(count // 128, 128),
+        parents,
+        inverses,
+        to_parent,
+        grandparent_factor,
+    )
+
+
+def general(loads, multipliers, gluing, signs, parents, inverses, to_parent, grandparent_factor):
     me = lax.axis_index("group")
     tree_depths = loads.shape[1]
     rows = loads.shape[2]
@@ -59,6 +345,11 @@
     return jnp.stack(solved)[None]
 
 
+def body(*args):
+    solved, flag = direct(*args)
+    return lax.cond(flag[HEAD - 1, 0] > 0, lambda: general(*args), lambda: solved)
+
+
 def solution(mesh):
     return jax.shard_map(
         body,

time: 622 us -> 122 us (0.20); the launches traced: 614 us -> 122 us
  waiting for transfers between devices: 502 us -> 0 us
  Pallas kernels: 0 us -> 104 us
  matrix products: 86.8 us -> 0 us
    all_gather x7 -> x0, waiting for transfers between devices: 386 us -> none  [body(): lax.all_gather(update_terms, 'group', axis=0, tiled=True)]
    reduce_scatter x1 -> x0, waiting for transfers between devices: 116 us -> none  [body(): lax.psum_scatter(jnp.dot(table, multipliers, precision=lax.Precision.HIGH...]
    pallas_call x0 -> x1, Pallas kernels: none -> 104 us  [direct(): pl.pallas_call(kernel, out_shape=(jax.ShapeDtypeStruct(loads.shape, f32),...]
    dot_general x23 -> x0, matrix products: 86.8 us -> none  [the longest x7 35.8 us: body(): jnp.einsum('km,kmbr->mbr', weight, lax.all_gather(update_terms, 'group',...]
  transfers between devices with their start and end apart: 8 -> 0, of which waited for: 8 -> 0; matrix products, arithmetic and copies ran while one was open for 1% -> 0% of each run, Pallas kernels for 0% -> 0%
where the time goes in v1:
time: 122 us
  Pallas kernels  104 us (85%)
  between operations  14 us (11%)
  local copies, waits for them, and re-layouts  3.55 us (3%)
    pallas_call x1, Pallas kernels, direct(): pl.pallas_call(kernel, out_shape=(jax.ShapeDtypeStruct(loads.shape, f32),...  104 us
    unnamed x2, local copies, waits for them, and re-layouts  3.03 us

profile of v1, /device:TPU:96, one launch (start us, length us, event | category | flops | bytes accessed | tf_op | source)
XLA Modules:
  0.0 122.0 jit_solution(7428950818722548526)
XLA Ops:
  6.5 0.8 copy.17.parents
  7.3 104.2 %shard_map.84 = (f32[1,8,128,256]{3,2,1,0:T(8,128)}, f32[8,128]{1,0:T(8,128)S(1)}) custom-call(f32[1,8,128,256]{3,2,1,0:T(8,128)} %loads.1, f32[512,256]{1,0:T(8,128)} %multipliers.1, s32[4,128]{1,0:T(4,128)} %bitcast.372, s32[4,128]{1,0:T(4,128)} %bitcast.365, s32[16,7]{1,0:T(8,128)S(1)} %copy.17.parents, f32[1,8,128,128]{3,2,1,0:T(8,128)} %inverses.1, ...), custom_call_target="tpu_custom_call" | custom-call | tf_op jit(solution)/shard_map/pallas_call | solution.py:241
  111.5 0.5 slice.177
  112.7 0.2 conditional.1
  112.9 2.3 %copy.88 = f32[1,8,128,256]{3,2,1,0:T(8,128)} copy(f32[1,8,128,256]{3,2,1,0:T(8,128)} %get-tuple-element.38) | data formatting | bytes 2097152

commit v2 on v1

--- a/solution.py
+++ b/solution.py
@@ -27,25 +27,109 @@
 def kernel(
     loads, multipliers, gluing, signs, parents, inverses, to_parent, grandparent,
     out, flag,
-    bucket, received, rows_high, rows_low, pending, parent_map,
-    inv_h, inv_l, one_h, one_l, two_h, two_l,
-    one_out, one_in, two_out, two_in, sum_out, sum_in, carried,
-    pack_send, pack_recv, one_send, one_recv, two_send, two_recv, sum_send, sum_recv,
+    bucket, received, rows_high, rows_low, pending, parent_map, child_map, near_map, far_map,
+    inv_h, inv_l, near_h, near_l, far_h, far_l, six_h, six_l, step_five,
+    up_out, up_in, down_out, down_in, item_out, item_in, root_out, root_in,
+    pack_send, pack_recv, up_send, up_recv, down_send, down_recv, item_send, item_recv, root_send, root_recv,
 ):
     nodes = parents.shape[0]
     levels, rows, columns = loads.shape[1:]
     count = multipliers.shape[0]
     me = lax.axis_index("group")
     others = nodes - 1
+    part = rows // nodes
+    rounds = levels // 2 - 1
+    blocks = (nodes, part, columns)
 
     def peer(k):
-        return lax.rem(me + k, nodes)
+        def shift(t):
+            return jnp.where(t < 2, t + 2, 3 - t)
+
+        y = lax.rem(lax.div(me, 4) + shift(lax.div(k, 4)), 4)
+        x = lax.rem(lax.rem(me, 4) + shift(lax.rem(k, 4)), 4)
+        return 4 * y + x
+
+    def copy(source, target, send, recv, device):
+        return pltpu.make_async_remote_copy(
+            src_ref=source,
+            dst_ref=target,
+            send_sem=send,
+            recv_sem=recv,
+            device_id={"group": device},
+            device_id_type=pl.DeviceIdType.MESH,
+        )
+
+    class Exchange:
+        def __init__(self, source, target, send, recv):
+            self.source, self.target, self.send, self.recv = source, target, send, recv
+
+        def start(self):
+            @pl.loop(0, others)
+            def _(k):
+                device = peer(k)
+                copy(self.source.at[device], self.target.at[me], self.send, self.recv, device).start()
+
+            self.target[me] = self.source[me]
+
+        def all(self):
+            most = pl.ds(0, others)
+            return copy(self.source.at[most], self.target.at[most], self.send, self.recv, peer(0))
+
+        def arrived(self):
+            self.all().wait_recv()
+
+        def sent(self):
+            self.all().wait_send()
+
+    def item(i):
+        return Exchange(item_out.at[i], item_in.at[i], item_send.at[i], item_recv.at[i])
+
+    pack = Exchange(bucket, received, pack_send.at[0], pack_recv.at[0])
+    up = [Exchange(up_out.at[r], up_in.at[r], up_send.at[r], up_recv.at[r]) for r in range(rounds)]
+    down = [Exchange(down_out.at[r], down_in.at[r], down_send.at[r], down_recv.at[r]) for r in range(rounds)]
+    step_up = [item(r) for r in range(rounds)]
+    step_down = [item(rounds + r) for r in range(rounds)]
+    ask_up = [item(2 * rounds + r) for r in range(rounds)]
+    ask_down = [item(3 * rounds + r) for r in range(rounds)]
+    tail_up = item(4 * rounds)
+    root_down = item(4 * rounds + 1)
+    root_up = Exchange(root_out, root_in, root_send.at[0], root_recv.at[0])
+    everything = [pack, *up, *down, *step_up, *step_down, *ask_up, *ask_down, tail_up, root_down, root_up]
 
     barrier = pltpu.get_barrier_semaphore()
 
-    @pl.loop(1, nodes)
+    @pl.loop(0, others)
     def _(k):
         pl.semaphore_signal(barrier, inc=1, device_id={"group": peer(k)}, device_id_type=pl.DeviceIdType.MESH)
+
+    def pair(level):
+        both = jnp.concatenate([to_parent[0, level], grandparent[0, level]], axis=0)
+        return product(split(both), inverses[0, level])
+
+    def ask(r, both):
+        near_h[r], near_l[r] = split(both)
+        item_out[2 * rounds + r] = jnp.concatenate([both[:rows], both[rows:]], axis=1).reshape(blocks)
+
+    ask(0, pair(1))
+
+    spread = lax.div(lax.broadcasted_iota(jnp.int32, (nodes, rows), 1), part)
+    spread = spread == lax.broadcasted_iota(jnp.int32, (nodes, rows), 0)
+    spread = jnp.where(spread, 1.0, 0.0).astype(jnp.bfloat16)
+    names = parents[...].astype(jnp.float32).astype(jnp.bfloat16)
+    over = (((0,), (0,)), ((), ()))
+    across = lax.dot_general(names, spread, over, preferred_element_type=jnp.float32).astype(jnp.int32)
+    along = lax.dot_general(spread, names, over, preferred_element_type=jnp.float32).astype(jnp.int32)
+    place_r = lax.broadcasted_iota(jnp.int32, (rows, rows), 0)
+    place_c = lax.broadcasted_iota(jnp.int32, (rows, rows), 1)
+    same = lax.rem(place_r, part) == lax.rem(place_c, part)
+    for l in range(levels - 1):
+        hit = same & (lax.div(place_r, part) == across[l : l + 1, :])
+        parent_map[l] = jnp.where(hit, 1.0, 0.0).astype(jnp.bfloat16)
+        hit = same & (lax.div(place_c, part) == along[:, l : l + 1])
+        child_map[l] = jnp.where(hit, 1.0, 0.0).astype(jnp.bfloat16)
+
+    pl.semaphore_wait(barrier, others)
+    ask_up[0].start()
 
     dof = jnp.concatenate([gluing[i : i + 1, :] for i in range(gluing.shape[0])], axis=1)
     sign = jnp.concatenate([signs[i : i + 1, :] for i in range(signs.shape[0])], axis=1)
@@ -55,13 +139,13 @@
     row = lax.rem(dof, span)
     order = lax.broadcasted_iota(jnp.int32, (1, count), 1)
     key = (dof * count + order).astype(jnp.float32)
-    start = (node * (span * count)).astype(jnp.float32)
+    first_key = (node * (span * count)).astype(jnp.float32)
     rank = jnp.zeros((1, count), jnp.float32)
     for i in range(count // 128):
         lanes = jnp.broadcast_to(key[:, i * 128 : (i + 1) * 128], (128, 128))
-        down = jnp.transpose(lanes)
-        down = jnp.concatenate([down] * (count // 128), axis=1)
-        before = (down < key) & (down >= start)
+        down_key = jnp.transpose(lanes)
+        down_key = jnp.concatenate([down_key] * (count // 128), axis=1)
+        before = (down_key < key) & (down_key >= first_key)
         rank = rank + jnp.sum(jnp.where(before, 1.0, 0.0), axis=0, keepdims=True)
     rank = rank.astype(jnp.int32)
     fits = rank < CHUNKS * SLOTS
@@ -90,60 +174,55 @@
         packed = mm(table, m_high) + mm(table, m_low)
         first = HEAD + j * SLOTS
         bucket[:, first : first + SLOTS, :] = packed.reshape(nodes, SLOTS, columns)
-
-    pl.semaphore_wait(barrier, others)
-
-    def copy(source, target, send, recv, k):
-        return pltpu.make_async_remote_copy(
-            src_ref=source,
-            dst_ref=target,
-            send_sem=send,
-            recv_sem=recv,
-            device_id={"group": peer(k)},
-            device_id_type=pl.DeviceIdType.MESH,
-        )
-
-    @pl.loop(1, nodes)
-    def _(k):
-        copy(bucket.at[peer(k)], received.at[me], pack_send.at[0], pack_recv.at[0], k).start()
-
-    received[me] = bucket[me]
+    pack.start()
+
+    ask(1, pair(3))
+    ask_up[1].start()
+    six = product(split(to_parent[0, levels - 2]), inverses[0, levels - 2])
+    six_h[...], six_l[...] = split(six)
+    root_out[...] = six.reshape(nodes, part, rows)
+    root_up.start()
+    step_five[...] = pair(5)
 
     @pl.loop(0, levels)
     def _(l):
         inv_h[l], inv_l[l] = split(inverses[0, l])
 
-    @pl.loop(0, levels - 1)
-    def _(l):
-        one_h[l], one_l[l] = split(to_parent[0, l])
-
-    @pl.loop(0, levels - 2)
-    def _(l):
-        two_h[l], two_l[l] = split(grandparent[0, l])
-
-    chunk_rows = rows // nodes
-    spread = lax.broadcasted_iota(jnp.int32, (nodes, rows), 1)
-    spread = lax.div(spread, chunk_rows) == lax.broadcasted_iota(jnp.int32, (nodes, rows), 0)
-    spread = jnp.where(spread, 1.0, 0.0).astype(jnp.bfloat16)
-    across = lax.dot_general(
-        parents[...].astype(jnp.float32).astype(jnp.bfloat16),
-        spread,
-        (((0,), (0,)), ((), ())),
-        preferred_element_type=jnp.float32,
-    )
-    down_rows = lax.broadcasted_iota(jnp.int32, (rows, rows), 0)
-    same = lax.rem(down_rows, chunk_rows) == lax.rem(
-        lax.broadcasted_iota(jnp.int32, (rows, rows), 1), chunk_rows
-    )
-    down_node = lax.div(down_rows, chunk_rows)
-    for l in range(levels - 1):
-        hit = same & (down_node == across[l : l + 1, :].astype(jnp.int32))
-        parent_map[l] = jnp.where(hit, 1.0, 0.0).astype(jnp.bfloat16)
-    carried[...] = jnp.zeros_like(carried)
-    sum_in[0] = jnp.zeros_like(sum_in[0])
-
-    copy(bucket.at[pl.ds(0, others)], received.at[pl.ds(0, others)], pack_send.at[0], pack_recv.at[0], 1).wait_recv()
-
+    def chain(a, b):
+        return mm(a, b).astype(jnp.bfloat16)
+
+    for r in range(rounds):
+        w0, w1, w2 = parent_map[2 * r], parent_map[2 * r + 1], parent_map[2 * r + 2]
+        near_map[r] = jnp.concatenate([w1, chain(w1, w0)], axis=1)
+        both = chain(w2, w1)
+        far_map[r] = jnp.concatenate([both, chain(both, w0), w2], axis=1)
+
+    def gather(table, values):
+        high, low = split(values)
+        return mm(table, high) + mm(table, low)
+
+    def answer(r):
+        ask_up[r].arrived()
+        found = gather(child_map[2 * r], item_in[2 * rounds + r].reshape(rows, columns))
+        item_out[3 * rounds + r] = found.reshape(blocks)
+        ask_down[r].start()
+
+    def compose(r):
+        ask_down[r].arrived()
+        found = item_in[3 * rounds + r].reshape(rows, columns)
+        found = jnp.concatenate([found[:, :rows], found[:, rows:]], axis=0)
+        step = to_parent[0, 2 * r]
+        leap = grandparent[0, 2 * r]
+        made = product(split(found), step)
+        far = -made[rows:]
+        if r == rounds - 1:
+            beyond = item_in[4 * rounds + 1].reshape(rows, columns)[:, rows:]
+            far = far - product(split(beyond), leap)
+        whole = jnp.concatenate([leap - made[:rows], far, step], axis=0)
+        far_h[r], far_l[r] = split(whole)
+
+    answer(0)
+    pack.arrived()
     head = received[0, 0:HEAD, :]
     for i in range(1, nodes):
         head = head + received[i, 0:HEAD, :]
@@ -162,70 +241,80 @@
         table = jnp.where(table, 1.0, 0.0).astype(jnp.bfloat16)
         pending[l] = loads[0, l] - (mm(table, rows_high[...]) + mm(table, rows_low[...]))
 
-    def send(l, source, target, send_sem, recv_sem):
-        @pl.loop(1, nodes)
-        def _(k):
-            copy(source.at[l, peer(k)], target.at[l, me], send_sem.at[l], recv_sem.at[l], k).start()
-
-        target[l, me] = source[l, me]
-
-    def arrived(l, source, target, send_sem, recv_sem):
-        copy(
-            source.at[l, pl.ds(0, others)], target.at[l, pl.ds(0, others)], send_sem.at[l], recv_sem.at[l], 1
-        ).wait_recv()
-
-    def sent(l, source, target, send_sem, recv_sem):
-        copy(
-            source.at[l, pl.ds(0, others)], target.at[l, pl.ds(0, others)], send_sem.at[l], recv_sem.at[l], 1
-        ).wait_send()
-
-    one = (one_out, one_in, one_send, one_recv)
-    two = (two_out, two_in, two_send, two_recv)
-    total = (sum_out, sum_in, sum_send, sum_recv)
-    blocks = (nodes, chunk_rows, columns)
-
-    def solve(l):
-        x = pending[l] - sum_in[l].reshape(rows, columns)
-        x = product((inv_h[l], inv_l[l]), x)
-        out[0, l] = x
+    compose(0)
+
+    def solve(level, x):
+        x = product((inv_h[level], inv_l[level]), x)
+        out[0, level] = x
         return x
 
-    @pl.loop(0, levels - 1)
-    def _(l):
-        x = solve(l)
-        one_out[l] = product((one_h[l], one_l[l]), x).reshape(blocks)
-        send(l, *one)
-
-        @pl.when(l < levels - 2)
-        def _():
-            two_out[l] = product((two_h[l], two_l[l]), x).reshape(blocks)
-            send(l, *two)
-
-        arrived(l, *one)
-        high, low = split(one_in[l].reshape(rows, columns) + carried[...])
-        sum_out[l + 1] = (mm(parent_map[l], high) + mm(parent_map[l], low)).reshape(blocks)
-        send(l + 1, *total)
-
-        @pl.when(l < levels - 2)
-        def _():
-            arrived(l, *two)
-            high, low = split(two_in[l].reshape(rows, columns))
-            carried[...] = mm(parent_map[l], high) + mm(parent_map[l], low)
-
-        arrived(l + 1, *total)
-
-    solve(levels - 1)
-
-    copy(bucket.at[pl.ds(0, others)], received.at[pl.ds(0, others)], pack_send.at[0], pack_recv.at[0], 1).wait_send()
-
-    @pl.loop(0, levels - 1)
-    def _(l):
-        sent(l, *one)
-        sent(l + 1, *total)
-
-    @pl.loop(0, levels - 2)
-    def _(l):
-        sent(l, *two)
+    def skipped(r):
+        step_down[r].arrived()
+        solve(2 * r + 1, pending[2 * r + 1] - item_in[rounds + r].reshape(rows, columns))
+
+    for r in range(rounds):
+        level = 2 * r
+        if r > 0:
+            pending[level] = pending[level] - down_in[r - 1, :, :part].reshape(rows, columns)
+            pending[level + 1] = pending[level + 1] - down_in[r - 1, :, part:].reshape(rows, columns)
+        e = product((near_h[r], near_l[r]), pending[level + 1])
+        up_out[r, :, 0:part] = e[:rows].reshape(blocks)
+        up_out[r, :, 2 * part : 3 * part] = e[rows:].reshape(blocks)
+        x = solve(level, pending[level])
+        c = product((far_h[r, : 2 * rows], far_l[r, : 2 * rows]), x)
+        up_out[r, :, part : 2 * part] = c[:rows].reshape(blocks)
+        up_out[r, :, 3 * part :] = c[rows:].reshape(blocks)
+        up[r].start()
+        item_out[r] = product((far_h[r, 2 * rows :], far_l[r, 2 * rows :]), x).reshape(blocks)
+        step_up[r].start()
+
+        if r == 0:
+            answer(1)
+            root_up.arrived()
+            six_in = root_in[...].reshape(rows, rows)
+            above = gather(child_map[5], six_in)
+            above = jnp.concatenate([above, gather(child_map[4], above)], axis=1)
+            item_out[4 * rounds + 1] = above.reshape(blocks)
+            root_down.start()
+            item_out[4 * rounds] = product((six_h[...], six_l[...]), pending[levels - 2]).reshape(blocks)
+            tail_up.start()
+        else:
+            skipped(r - 1)
+        if r == 1:
+            answer(2)
+
+        up[r].arrived()
+        first = jnp.concatenate([up_in[r, :, i * part : (i + 1) * part].reshape(rows, columns) for i in (0, 1)], axis=0)
+        down_out[r, :, :part] = gather(near_map[r], first).reshape(blocks)
+        second = jnp.concatenate([up_in[r, :, i * part : (i + 1) * part].reshape(rows, columns) for i in (2, 3)], axis=0)
+        if r == rounds - 1:
+            tail_up.arrived()
+            second = jnp.concatenate([second, item_in[4 * rounds].reshape(rows, columns)], axis=0)
+            second = gather(far_map[r], second)
+        else:
+            second = gather(far_map[r, :, : 2 * rows], second)
+        down_out[r, :, part:] = second.reshape(blocks)
+        down[r].start()
+        step_up[r].arrived()
+        item_out[rounds + r] = gather(parent_map[level], item_in[r].reshape(rows, columns)).reshape(blocks)
+        step_down[r].start()
+
+        if r == 0:
+            root_down.arrived()
+            beyond = item_in[4 * rounds + 1].reshape(rows, columns)[:, :rows]
+            five = step_five[...]
+            ask(2, jnp.concatenate([five[:rows], five[rows:] - product(split(beyond), five[:rows])], axis=0))
+            ask_up[2].start()
+        if r < rounds - 1:
+            compose(r + 1)
+        down[r].arrived()
+
+    solve(levels - 2, pending[levels - 2] - down_in[rounds - 1, :, :part].reshape(rows, columns))
+    solve(levels - 1, pending[levels - 1] - down_in[rounds - 1, :, part:].reshape(rows, columns))
+    skipped(rounds - 1)
+
+    for exchange in everything:
+        exchange.sent()
 
 
 def direct(loads, multipliers, gluing, signs, parents, inverses, to_parent, grandparent_factor):
@@ -234,8 +323,9 @@
     count = multipliers.shape[0]
     f32, bf16 = jnp.float32, jnp.bfloat16
     room = HEAD + CHUNKS * SLOTS
-    blocks = (nodes, rows // nodes, columns)
-    square = (rows, rows)
+    rounds = levels // 2 - 1
+    part = rows // nodes
+    items = 4 * rounds + 2
     dma = pltpu.SemaphoreType.DMA
     vmem = pl.BlockSpec(memory_space=pltpu.VMEM)
     return pl.pallas_call(
@@ -252,28 +342,37 @@
             pltpu.VMEM((nodes * CHUNKS * SLOTS, columns), bf16),
             pltpu.VMEM((nodes * CHUNKS * SLOTS, columns), bf16),
             pltpu.VMEM((levels, rows, columns), f32),
-            pltpu.VMEM((levels - 1, *square), bf16),
-            pltpu.VMEM((levels, *square), bf16),
-            pltpu.VMEM((levels, *square), bf16),
-            pltpu.VMEM((levels - 1, *square), bf16),
-            pltpu.VMEM((levels - 1, *square), bf16),
-            pltpu.VMEM((levels - 2, *square), bf16),
-            pltpu.VMEM((levels - 2, *square), bf16),
-            pltpu.VMEM((levels - 1, *blocks), f32),
-            pltpu.VMEM((levels - 1, *blocks), f32),
-            pltpu.VMEM((levels - 2, *blocks), f32),
-            pltpu.VMEM((levels - 2, *blocks), f32),
-            pltpu.VMEM((levels, *blocks), f32),
-            pltpu.VMEM((levels, *blocks), f32),
-            pltpu.VMEM((rows, columns), f32),
+            pltpu.VMEM((levels - 1, rows, rows), bf16),
+            pltpu.VMEM((levels - 1, rows, rows), bf16),
+            pltpu.VMEM((rounds, rows, 2 * rows), bf16),
+            pltpu.VMEM((rounds, rows, 3 * rows), bf16),
+            pltpu.VMEM((levels, rows, rows), bf16),
+            pltpu.VMEM((levels, rows, rows), bf16),
+            pltpu.VMEM((rounds, 2 * rows, rows), bf16),
+            pltpu.VMEM((rounds, 2 * rows, rows), bf16),
+            pltpu.VMEM((rounds, 3 * rows, rows), bf16),
+            pltpu.VMEM((rounds, 3 * rows, rows), bf16),
+            pltpu.VMEM((rows, rows), bf16),
+            pltpu.VMEM((rows, rows), bf16),
+            pltpu.VMEM((2 * rows, rows), f32),
+            pltpu.VMEM((rounds, nodes, 4 * part, columns), f32),
+            pltpu.VMEM((rounds, nodes, 4 * part, columns), f32),
+            pltpu.VMEM((rounds, nodes, 2 * part, columns), f32),
+            pltpu.VMEM((rounds, nodes, 2 * part, columns), f32),
+            pltpu.VMEM((items, nodes, part, columns), f32),
+            pltpu.VMEM((items, nodes, part, columns), f32),
+            pltpu.VMEM((nodes, part, rows), f32),
+            pltpu.VMEM((nodes, part, rows), f32),
             dma((1,)),
             dma((1,)),
-            dma((levels - 1,)),
-            dma((levels - 1,)),
-            dma((levels - 2,)),
-            dma((levels - 2,)),
-            dma((levels,)),
-            dma((levels,)),
+            dma((rounds,)),
+            dma((rounds,)),
+            dma((rounds,)),
+            dma((rounds,)),
+            dma((items,)),
+            dma((items,)),
+            dma((1,)),
+            dma((1,)),
         ],
         compiler_params=pltpu.CompilerParams(
             collective_id=0, has_side_effects=True, vmem_limit_bytes=48 * 1024 * 1024

time: 122 us -> 98 us (0.80)
  Pallas kernels: 104 us -> 79.7 us
    pallas_call x1, Pallas kernels: 104 us -> 79.7 us  [direct(): pl.pallas_call(kernel, out_shape=(jax.ShapeDtypeStruct(loads.shape, f32),...]
where the time goes in v2:
time: 98 us; the launch traced here: 97.5 us
  Pallas kernels  79.7 us (81%)
  between operations  14 us (14%)
  local copies, waits for them, and re-layouts  3.55 us (4%)
    pallas_call x1, Pallas kernels, direct(): pl.pallas_call(kernel, out_shape=(jax.ShapeDtypeStruct(loads.shape, f32),...  79.7 us
    unnamed x2, local copies, waits for them, and re-layouts  3.03 us

profile of v2, /device:TPU:96, one launch (start us, length us, event | category | flops | bytes accessed | tf_op | source)
XLA Modules:
  0.0 97.5 jit_solution(1175123367478880425)
XLA Ops:
  6.5 0.8 copy.17.parents
  7.3 79.7 %shard_map.84 = (f32[1,8,128,256]{3,2,1,0:T(8,128)}, f32[8,128]{1,0:T(8,128)S(1)}) custom-call(f32[1,8,128,256]{3,2,1,0:T(8,128)} %loads.1, f32[512,256]{1,0:T(8,128)} %multipliers.1, s32[4,128]{1,0:T(4,128)} %bitcast.372, s32[4,128]{1,0:T(4,128)} %bitcast.365, s32[16,7]{1,0:T(8,128)S(1)} %copy.17.parents, f32[1,8,128,128]{3,2,1,0:T(8,128)} %inverses.1, ...), custom_call_target="tpu_custom_call" | custom-call | tf_op jit(solution)/shard_map/pallas_call | solution.py:331
  87.0 0.5 slice.177
  88.1 0.2 conditional.1
  88.4 2.3 %copy.88 = f32[1,8,128,256]{3,2,1,0:T(8,128)} copy(f32[1,8,128,256]{3,2,1,0:T(8,128)} %get-tuple-element.38) | data formatting | bytes 2097152

commit v3 on v2

--- a/solution.py
+++ b/solution.py
@@ -8,6 +8,7 @@
 CHUNKS = 4
 SLOTS = 16
 HEAD = 8
+EARLY = 2
 
 
 def split(x):
@@ -19,20 +20,25 @@
     return jnp.dot(a, b, preferred_element_type=jnp.float32)
 
 
+def halves(matrix):
+    return jnp.concatenate(split(matrix), axis=1)
+
+
 def product(matrix, x):
     high, low = split(x)
-    return mm(matrix[0], high) + (mm(matrix[0], low) + mm(matrix[1], high))
+    return mm(matrix, jnp.concatenate([high, high], axis=0)) + mm(matrix[:, : matrix.shape[1] // 2], low)
 
 
 def kernel(
-    loads, multipliers, gluing, signs, parents, inverses, to_parent, grandparent,
+    loads_hbm, multipliers_hbm, gluing_hbm, signs_hbm, parents_hbm, inverses_hbm, to_parent_hbm, grandparent_hbm,
     out, flag,
-    bucket, received, rows_high, rows_low, pending, parent_map, child_map, near_map, far_map,
-    inv_h, inv_l, near_h, near_l, far_h, far_l, six_h, six_l, step_five,
+    loads, multipliers, gluing, signs, parents, inverses, to_parent, grandparent, fetched,
+    bucket, received, late_bucket, late_received, rows_high, rows_low, pending, parent_map, child_map, near_map, far_map,
+    inverse, near, far, six, step_five,
     up_out, up_in, down_out, down_in, item_out, item_in, root_out, root_in,
     pack_send, pack_recv, up_send, up_recv, down_send, down_recv, item_send, item_recv, root_send, root_recv,
 ):
-    nodes = parents.shape[0]
+    nodes = parents.shape[1]
     levels, rows, columns = loads.shape[1:]
     count = multipliers.shape[0]
     me = lax.axis_index("group")
@@ -40,6 +46,20 @@
     part = rows // nodes
     rounds = levels // 2 - 1
     blocks = (nodes, part, columns)
+
+    arguments = (
+        (parents_hbm, parents),
+        (to_parent_hbm, to_parent),
+        (grandparent_hbm, grandparent),
+        (inverses_hbm, inverses),
+        (gluing_hbm, gluing),
+        (signs_hbm, signs),
+        (multipliers_hbm, multipliers),
+        (loads_hbm, loads),
+    )
+    fetches = [pltpu.make_async_copy(far, near, fetched.at[i]) for i, (far, near) in enumerate(arguments)]
+    for fetch in fetches:
+        fetch.start()
 
     def peer(k):
         def shift(t):
@@ -85,6 +105,7 @@
         return Exchange(item_out.at[i], item_in.at[i], item_send.at[i], item_recv.at[i])
 
     pack = Exchange(bucket, received, pack_send.at[0], pack_recv.at[0])
+    late_pack = Exchange(late_bucket, late_received, pack_send.at[1], pack_recv.at[1])
     up = [Exchange(up_out.at[r], up_in.at[r], up_send.at[r], up_recv.at[r]) for r in range(rounds)]
     down = [Exchange(down_out.at[r], down_in.at[r], down_send.at[r], down_recv.at[r]) for r in range(rounds)]
     step_up = [item(r) for r in range(rounds)]
@@ -94,7 +115,7 @@
     tail_up = item(4 * rounds)
     root_down = item(4 * rounds + 1)
     root_up = Exchange(root_out, root_in, root_send.at[0], root_recv.at[0])
-    everything = [pack, *up, *down, *step_up, *step_down, *ask_up, *ask_down, tail_up, root_down, root_up]
+    everything = [pack, late_pack, *up, *down, *step_up, *step_down, *ask_up, *ask_down, tail_up, root_down, root_up]
 
     barrier = pltpu.get_barrier_semaphore()
 
@@ -104,20 +125,20 @@
 
     def pair(level):
         both = jnp.concatenate([to_parent[0, level], grandparent[0, level]], axis=0)
-        return product(split(both), inverses[0, level])
+        return product(halves(both), inverses[0, level])
 
     def ask(r, both):
-        near_h[r], near_l[r] = split(both)
+        near[r] = halves(both)
         item_out[2 * rounds + r] = jnp.concatenate([both[:rows], both[rows:]], axis=1).reshape(blocks)
 
-    ask(0, pair(1))
+    fetches[0].wait()
 
     spread = lax.div(lax.broadcasted_iota(jnp.int32, (nodes, rows), 1), part)
     spread = spread == lax.broadcasted_iota(jnp.int32, (nodes, rows), 0)
     spread = jnp.where(spread, 1.0, 0.0).astype(jnp.bfloat16)
     names = parents[...].astype(jnp.float32).astype(jnp.bfloat16)
-    over = (((0,), (0,)), ((), ()))
-    across = lax.dot_general(names, spread, over, preferred_element_type=jnp.float32).astype(jnp.int32)
+    over = (((0,), (1,)), ((), ()))
+    across = mm(names, spread).astype(jnp.int32)
     along = lax.dot_general(spread, names, over, preferred_element_type=jnp.float32).astype(jnp.int32)
     place_r = lax.broadcasted_iota(jnp.int32, (rows, rows), 0)
     place_c = lax.broadcasted_iota(jnp.int32, (rows, rows), 1)
@@ -128,8 +149,13 @@
         hit = same & (lax.div(place_c, part) == along[:, l : l + 1])
         child_map[l] = jnp.where(hit, 1.0, 0.0).astype(jnp.bfloat16)
 
+    for fetch in fetches[1:4]:
+        fetch.wait()
+    ask(0, pair(1))
     pl.semaphore_wait(barrier, others)
     ask_up[0].start()
+    for fetch in fetches[4:6]:
+        fetch.wait()
 
     dof = jnp.concatenate([gluing[i : i + 1, :] for i in range(gluing.shape[0])], axis=1)
     sign = jnp.concatenate([signs[i : i + 1, :] for i in range(signs.shape[0])], axis=1)
@@ -151,7 +177,8 @@
     fits = rank < CHUNKS * SLOTS
     chunk = lax.div(rank, SLOTS)
     slot = lax.rem(rank, SLOTS)
-    overflow = jnp.max(jnp.where(fits, 0.0, 1.0))
+    fine = fits & ((row >= 2 * rows) | (chunk < EARLY))
+    overflow = jnp.max(jnp.where(fine, 0.0, 1.0))
 
     place = jnp.where(fits, node * HEAD + chunk, -1)
     owner_rows = lax.broadcasted_iota(jnp.int32, (nodes * HEAD, count), 0) == place
@@ -167,26 +194,29 @@
     bucket[:, 0:HEAD, :] = header.reshape(nodes, HEAD, columns)
 
     target = jnp.where(fits, chunk * (nodes * SLOTS) + node * SLOTS + slot, -1)
+    fetches[6].wait()
     m_high, m_low = split(multipliers[...])
-    for j in range(CHUNKS):
+
+    def packed(j):
         index = lax.broadcasted_iota(jnp.int32, (nodes * SLOTS, count), 0) + j * nodes * SLOTS
         table = jnp.where(index == target, coeff, 0.0).astype(jnp.bfloat16)
-        packed = mm(table, m_high) + mm(table, m_low)
-        first = HEAD + j * SLOTS
-        bucket[:, first : first + SLOTS, :] = packed.reshape(nodes, SLOTS, columns)
+        return (mm(table, m_high) + mm(table, m_low)).reshape(nodes, SLOTS, columns)
+
+    for j in range(EARLY):
+        bucket[:, HEAD + j * SLOTS : HEAD + (j + 1) * SLOTS, :] = packed(j)
     pack.start()
+    for j in range(CHUNKS - EARLY):
+        late_bucket[:, j * SLOTS : (j + 1) * SLOTS, :] = packed(EARLY + j)
 
     ask(1, pair(3))
-    ask_up[1].start()
-    six = product(split(to_parent[0, levels - 2]), inverses[0, levels - 2])
-    six_h[...], six_l[...] = split(six)
-    root_out[...] = six.reshape(nodes, part, rows)
-    root_up.start()
+    last_step = product(halves(to_parent[0, levels - 2]), inverses[0, levels - 2])
+    six[...] = halves(last_step)
+    root_out[...] = last_step.reshape(nodes, part, rows)
     step_five[...] = pair(5)
 
     @pl.loop(0, levels)
     def _(l):
-        inv_h[l], inv_l[l] = split(inverses[0, l])
+        inverse[l] = halves(inverses[0, l])
 
     def chain(a, b):
         return mm(a, b).astype(jnp.bfloat16)
@@ -213,38 +243,48 @@
         found = jnp.concatenate([found[:, :rows], found[:, rows:]], axis=0)
         step = to_parent[0, 2 * r]
         leap = grandparent[0, 2 * r]
-        made = product(split(found), step)
-        far = -made[rows:]
+        made = product(halves(found), step)
+        remote = -made[rows:]
         if r == rounds - 1:
             beyond = item_in[4 * rounds + 1].reshape(rows, columns)[:, rows:]
-            far = far - product(split(beyond), leap)
-        whole = jnp.concatenate([leap - made[:rows], far, step], axis=0)
-        far_h[r], far_l[r] = split(whole)
+            remote = remote - product(halves(beyond), leap)
+        far[r] = halves(jnp.concatenate([leap - made[:rows], remote, step], axis=0))
 
     answer(0)
+    late_pack.start()
+    ask_up[1].start()
+    root_up.start()
+
+    width = nodes * SLOTS
+
+    def unpack(j, values):
+        high, low = split(values.reshape(width, columns))
+        rows_high[j * width : (j + 1) * width] = high
+        rows_low[j * width : (j + 1) * width] = low
+
+    def glue(level, chunks, wanted):
+        table = lax.broadcasted_iota(jnp.int32, (rows, chunks * width), 0) + level * rows == wanted
+        table = jnp.where(table, 1.0, 0.0).astype(jnp.bfloat16)
+        glued = mm(table, rows_high[: chunks * width]) + mm(table, rows_low[: chunks * width])
+        pending[level] = loads[0, level] - glued
+
+    fetches[7].wait()
     pack.arrived()
     head = received[0, 0:HEAD, :]
     for i in range(1, nodes):
         head = head + received[i, 0:HEAD, :]
-    flag[...] = head[:, 0:128]
-    width = nodes * SLOTS
-    for j in range(CHUNKS):
-        first = HEAD + j * SLOTS
-        high, low = split(received[:, first : first + SLOTS, :].reshape(width, columns))
-        rows_high[j * width : (j + 1) * width] = high
-        rows_low[j * width : (j + 1) * width] = low
+    flag[0, 0] = jnp.where(jnp.max(head[HEAD - 1 :, :]) > 0.0, 1, 0)
     wanted = jnp.concatenate([head[j : j + 1, :] for j in range(CHUNKS)], axis=1).astype(jnp.int32)
-
-    @pl.loop(0, levels)
-    def _(l):
-        table = lax.broadcasted_iota(jnp.int32, (rows, CHUNKS * width), 0) + l * rows == wanted
-        table = jnp.where(table, 1.0, 0.0).astype(jnp.bfloat16)
-        pending[l] = loads[0, l] - (mm(table, rows_high[...]) + mm(table, rows_low[...]))
+    for j in range(EARLY):
+        unpack(j, received[:, HEAD + j * SLOTS : HEAD + (j + 1) * SLOTS, :])
+
+    for l in range(2):
+        glue(l, EARLY, wanted[:, : EARLY * width])
 
     compose(0)
 
     def solve(level, x):
-        x = product((inv_h[level], inv_l[level]), x)
+        x = product(inverse[level], x)
         out[0, level] = x
         return x
 
@@ -257,26 +297,34 @@
         if r > 0:
             pending[level] = pending[level] - down_in[r - 1, :, :part].reshape(rows, columns)
             pending[level + 1] = pending[level + 1] - down_in[r - 1, :, part:].reshape(rows, columns)
-        e = product((near_h[r], near_l[r]), pending[level + 1])
+        e = product(near[r], pending[level + 1])
         up_out[r, :, 0:part] = e[:rows].reshape(blocks)
         up_out[r, :, 2 * part : 3 * part] = e[rows:].reshape(blocks)
         x = solve(level, pending[level])
-        c = product((far_h[r, : 2 * rows], far_l[r, : 2 * rows]), x)
+        c = product(far[r, : 2 * rows], x)
         up_out[r, :, part : 2 * part] = c[:rows].reshape(blocks)
         up_out[r, :, 3 * part :] = c[rows:].reshape(blocks)
         up[r].start()
-        item_out[r] = product((far_h[r, 2 * rows :], far_l[r, 2 * rows :]), x).reshape(blocks)
+        item_out[r] = product(far[r, 2 * rows :], x).reshape(blocks)
         step_up[r].start()
 
         if r == 0:
             answer(1)
+            late_pack.arrived()
+            for j in range(CHUNKS - EARLY):
+                unpack(EARLY + j, late_received[:, j * SLOTS : (j + 1) * SLOTS, :])
+
+            @pl.loop(2, levels)
+            def _(l):
+                glue(l, CHUNKS, wanted)
+
             root_up.arrived()
             six_in = root_in[...].reshape(rows, rows)
             above = gather(child_map[5], six_in)
             above = jnp.concatenate([above, gather(child_map[4], above)], axis=1)
             item_out[4 * rounds + 1] = above.reshape(blocks)
             root_down.start()
-            item_out[4 * rounds] = product((six_h[...], six_l[...]), pending[levels - 2]).reshape(blocks)
+            item_out[4 * rounds] = product(six[...], pending[levels - 2]).reshape(blocks)
             tail_up.start()
         else:
             skipped(r - 1)
@@ -303,7 +351,7 @@
             root_down.arrived()
             beyond = item_in[4 * rounds + 1].reshape(rows, columns)[:, :rows]
             five = step_five[...]
-            ask(2, jnp.concatenate([five[:rows], five[rows:] - product(split(beyond), five[:rows])], axis=0))
+            ask(2, jnp.concatenate([five[:rows], five[rows:] - product(halves(beyond), five[:rows])], axis=0))
             ask_up[2].start()
         if r < rounds - 1:
             compose(r + 1)
@@ -322,7 +370,7 @@
     _, levels, rows, columns = loads.shape
     count = multipliers.shape[0]
     f32, bf16 = jnp.float32, jnp.bfloat16
-    room = HEAD + CHUNKS * SLOTS
+    room = HEAD + EARLY * SLOTS
     rounds = levels // 2 - 1
     part = rows // nodes
     items = 4 * rounds + 2
@@ -332,13 +380,24 @@
         kernel,
         out_shape=(
             jax.ShapeDtypeStruct(loads.shape, f32),
-            jax.ShapeDtypeStruct((HEAD, 128), f32),
+            jax.ShapeDtypeStruct((1, 1), jnp.int32),
         ),
-        in_specs=[vmem] * 8,
-        out_specs=(vmem, vmem),
+        in_specs=[pl.BlockSpec(memory_space=pltpu.HBM)] * 8,
+        out_specs=(vmem, pl.BlockSpec(memory_space=pltpu.SMEM)),
         scratch_shapes=[
+            pltpu.VMEM(loads.shape, f32),
+            pltpu.VMEM(multipliers.shape, f32),
+            pltpu.VMEM((count // 128, 128), jnp.int32),
+            pltpu.VMEM((count // 128, 128), jnp.int32),
+            pltpu.VMEM((levels - 1, nodes), jnp.int32),
+            pltpu.VMEM(inverses.shape, f32),
+            pltpu.VMEM(to_parent.shape, f32),
+            pltpu.VMEM(grandparent_factor.shape, f32),
+            dma((8,)),
             pltpu.VMEM((nodes, room, columns), f32),
             pltpu.VMEM((nodes, room, columns), f32),
+            pltpu.VMEM((nodes, (CHUNKS - EARLY) * SLOTS, columns), f32),
+            pltpu.VMEM((nodes, (CHUNKS - EARLY) * SLOTS, columns), f32),
             pltpu.VMEM((nodes * CHUNKS * SLOTS, columns), bf16),
             pltpu.VMEM((nodes * CHUNKS * SLOTS, columns), bf16),
             pltpu.VMEM((levels, rows, columns), f32),
@@ -346,14 +405,10 @@
             pltpu.VMEM((levels - 1, rows, rows), bf16),
             pltpu.VMEM((rounds, rows, 2 * rows), bf16),
             pltpu.VMEM((rounds, rows, 3 * rows), bf16),
-            pltpu.VMEM((levels, rows, rows), bf16),
-            pltpu.VMEM((levels, rows, rows), bf16),
-            pltpu.VMEM((rounds, 2 * rows, rows), bf16),
-            pltpu.VMEM((rounds, 2 * rows, rows), bf16),
-            pltpu.VMEM((rounds, 3 * rows, rows), bf16),
-            pltpu.VMEM((rounds, 3 * rows, rows), bf16),
-            pltpu.VMEM((rows, rows), bf16),
-            pltpu.VMEM((rows, rows), bf16),
+            pltpu.VMEM((levels, rows, 2 * rows), bf16),
+            pltpu.VMEM((rounds, 2 * rows, 2 * rows), bf16),
+            pltpu.VMEM((rounds, 3 * rows, 2 * rows), bf16),
+            pltpu.VMEM((rows, 2 * rows), bf16),
             pltpu.VMEM((2 * rows, rows), f32),
             pltpu.VMEM((rounds, nodes, 4 * part, columns), f32),
             pltpu.VMEM((rounds, nodes, 4 * part, columns), f32),
@@ -363,8 +418,8 @@
             pltpu.VMEM((items, nodes, part, columns), f32),
             pltpu.VMEM((nodes, part, rows), f32),
             pltpu.VMEM((nodes, part, rows), f32),
-            dma((1,)),
-            dma((1,)),
+            dma((2,)),
+            dma((2,)),
             dma((rounds,)),
             dma((rounds,)),
             dma((rounds,)),
@@ -382,7 +437,7 @@
         multipliers,
         gluing.reshape(count // 128, 128),
         signs.reshape(count // 128, 128),
-        parents,
+        parents.T,
         inverses,
         to_parent,
         grandparent_factor,
@@ -391,62 +446,77 @@
 
 def general(loads, multipliers, gluing, signs, parents, inverses, to_parent, grandparent_factor):
     me = lax.axis_index("group")
-    tree_depths = loads.shape[1]
-    rows = loads.shape[2]
-    span = tree_depths * rows
+    size = lax.axis_size("group")
+    levels, rows, columns = loads.shape[1:]
+    span = levels * rows
+    ring = [(i, (i + 1) % size) for i in range(size)]
+    exact = lax.Precision.HIGHEST
+
+    def passed(value):
+        return lax.ppermute(value, "group", ring)
+
+    target = (me * span + lax.iota(jnp.int32, span)).astype(jnp.float32)
+
+    def add(_, state):
+        glued, values, at = state
+        table = jnp.where(target[:, None] == at[None, :], 1.0, 0.0)
+        glued = glued + jnp.dot(table, values, precision=exact)
+        return glued, passed(values), passed(at)
+
     coeff = (2 * signs - 1).astype(jnp.float32)
-    target = lax.iota(jnp.int32, lax.axis_size("group") * span)
-    table = jnp.where(target[:, None] == gluing[None, :], coeff[None, :], 0.0)
-    glued = lax.psum_scatter(
-        jnp.dot(
-            table, multipliers, precision=lax.Precision.HIGHEST, preferred_element_type=jnp.float32
-        ),
-        "group",
-        scatter_dimension=0,
-        tiled=True,
-    )
-    awaiting_contribution = [
-        loads[0, level] - glued[level * rows : (level + 1) * rows] for level in range(tree_depths)
-    ]
-    node_count = parents.shape[0]
-    solved = []
-    for level in range(tree_depths):
-        unknown_estimate = jnp.dot(
-            inverses[0, level],
-            awaiting_contribution[level],
-            precision=lax.Precision.HIGHEST,
-            preferred_element_type=jnp.float32,
-        )
-        solved.append(unknown_estimate)
-        if level + 1 < tree_depths:
-            first = parents[:, level]
-            if level + 2 < tree_depths:
-                match = first[:, None] == lax.iota(jnp.int32, node_count)[None, :]
-                second_term = jnp.sum(jnp.where(match, parents[None, :, level + 1], 0), axis=1)
-                targets = jnp.stack([first, second_term], axis=1)
-                panel_sequence = jnp.stack([to_parent[0, level], grandparent_factor[0, level]])
-            else:
-                targets = first[:, None]
-                panel_sequence = to_parent[0, level][None]
-            update_terms = jnp.einsum(
-                "xdf,fh->xdh", panel_sequence, unknown_estimate, precision=lax.Precision.HIGHEST
-            )[None]
-            weight = (targets == me).astype(jnp.float32)
-            moved = jnp.einsum(
-                "km,kmbr->mbr",
-                weight,
-                lax.all_gather(update_terms, "group", axis=0, tiled=True),
-                precision=lax.Precision.HIGHEST,
-            )
-            awaiting_contribution[level + 1] = awaiting_contribution[level + 1] - moved[0]
-            if level + 2 < tree_depths:
-                awaiting_contribution[level + 2] = awaiting_contribution[level + 2] - moved[1]
-    return jnp.stack(solved)[None]
+    start = (jnp.zeros((span, columns), jnp.float32), coeff[:, None] * multipliers, gluing.astype(jnp.float32))
+    glued = lax.fori_loop(0, size, add, start)[0]
+    pending = loads[0] - glued.reshape(levels, rows, columns)
+    pending = jnp.concatenate([pending, jnp.zeros((2, rows, columns), jnp.float32)])
+    one = jnp.concatenate([to_parent[0], jnp.zeros((1, rows, rows), jnp.float32)])
+    two = jnp.concatenate([grandparent_factor[0], jnp.zeros((2, rows, rows), jnp.float32)])
+    firsts = jnp.concatenate([parents, jnp.zeros((size, 2), jnp.int32)], axis=1)
+
+    def level(l, state):
+        pending, solved = state
+        x = jnp.dot(inverses[0, l], pending[l], precision=exact)
+        solved = solved.at[l].set(x)
+        first = firsts[:, l]
+        second = firsts[first, l + 1]
+
+        def take(s, state):
+            here, there, up, leap = state
+            source = lax.rem(me - s + size, size)
+            here = here + jnp.where(first[source] == me, up, 0.0)
+            there = there + jnp.where(second[source] == me, leap, 0.0)
+            return here, there, passed(up), passed(leap)
+
+        zero = jnp.zeros((rows, columns), jnp.float32)
+        up = jnp.dot(one[l], x, precision=exact)
+        leap = jnp.dot(two[l], x, precision=exact)
+        here, there, _, _ = lax.fori_loop(0, size, take, (zero, zero, up, leap))
+        return pending.at[l + 1].add(-here).at[l + 2].add(-there), solved
+
+    solved = lax.fori_loop(0, levels, level, (pending, jnp.zeros(loads.shape[1:], jnp.float32)))[1]
+    return solved[None]
+
+
+def finish_kernel(source, target, done):
+    pieces = [pltpu.make_async_copy(source.at[0, l], target.at[0, l], done.at[l]) for l in range(source.shape[1])]
+    for piece in pieces:
+        piece.start()
+    for piece in pieces:
+        piece.wait()
+
+
+def finish(solved):
+    return pl.pallas_call(
+        finish_kernel,
+        out_shape=jax.ShapeDtypeStruct(solved.shape, solved.dtype),
+        in_specs=[pl.BlockSpec(memory_space=pltpu.VMEM)],
+        out_specs=pl.BlockSpec(memory_space=pl.ANY),
+        scratch_shapes=[pltpu.SemaphoreType.DMA((solved.shape[1],))],
+    )(solved)
 
 
 def body(*args):
     solved, flag = direct(*args)
-    return lax.cond(flag[HEAD - 1, 0] > 0, lambda: general(*args), lambda: solved)
+    return lax.cond(flag[0, 0] != 0, lambda: general(*args), lambda: finish(solved))
 
 
 def solution(mesh):

time: 98 us -> 75.3 us (0.77)
  between operations: 14 us -> 0.89 us
  Pallas kernels: 79.7 us -> 74.1 us
  local copies, waits for them, and re-layouts: 3.55 us -> 0.03 us
    pallas_call x1, Pallas kernels: 79.7 us -> 73.1 us  [direct(): pl.pallas_call(kernel, out_shape=(jax.ShapeDtypeStruct(loads.shape, f32),...]
    unnamed x2 -> x14, local copies, waits for them, and re-layouts: 3.03 us -> 0.03 us
    pallas_call x0 -> x1, Pallas kernels: none -> 1.03 us  [finish(): pl.pallas_call(finish_kernel, out_shape=jax.ShapeDtypeStruct(solved.shape...]
where the time goes in v3:
time: 75.3 us
  Pallas kernels  74.1 us (98%)
  between operations  0.89 us (1%)
    pallas_call x1, Pallas kernels, direct(): pl.pallas_call(kernel, out_shape=(jax.ShapeDtypeStruct(loads.shape, f32),...  73.1 us

profile of v3, /device:TPU:96, one launch (start us, length us, event | category | flops | bytes accessed | tf_op | source)
XLA Modules:
  0.0 75.3 jit_solution(5257091150922101412)
XLA Ops:
  0.0 0.0 copy-start
  0.0 0.0 copy-start.1
  0.0 0.0 copy-start.2
  0.0 0.0 copy-start.3
  0.0 0.0 copy-start.4
  0.0 0.0 copy-start.7
  0.0 0.0 copy-start.8
  0.0 73.1 %shard_map.84 = (f32[1,8,128,256]{3,2,1,0:T(8,128)S(1)}, s32[1,1]{1,0:T(1,128)}) custom-call(f32[1,8,128,256]{3,2,1,0:T(8,128)} %loads_hbm.1, f32[512,256]{1,0:T(8,128)} %multipliers_hbm.1, s32[4,128]{1,0:T(4,128)} %bitcast.82, s32[4,128]{1,0:T(4,128)} %bitcast.83, s32[7,16]{1,0:T(8,128)} %bitcast.81, f32[1,8,128,128]{3,2,1,0:T(8,128)} %inverses_hbm.1, ...), custom_call_target="tpu_custom_call" | custom-call | tf_op jit(solution)/shard_map/pallas_call | solution.py:379
  73.8 0.0 copy-done
  73.8 0.0 copy-done.1
  73.8 0.0 copy-done.2
  73.8 0.0 copy-done.3
  73.8 0.0 copy-done.4
  73.8 0.0 copy-done.7
  73.9 0.0 copy-done.8
  73.9 1.2 %conditional.1 = (f32[1,8,128,256]{3,2,1,0:T(8,128)}) conditional(s32[]{:T(128)} %bitcast.20, f32[1,8,128,256]{3,2,1,0:T(8,128)S(1)} %get-tuple-element.489, (f32[1,8,128,256]{3,2,1,0:T(8,128)S(1)}, s32[512]{0:T(512)S(1)}, f32[512,256]{1,0:T(8,128)S(1)}, s32[512]{0:T(512)S(1)}, s32[16,7]{0,1:T(8,128)S(1)}, ...), branch_computations={%region_0.0_spmd, %region_1.11_spmd} | conditional | flops 1764003968 | bytes 19699634 | solution.py:519
  73.9 1.0 %branch_0_fun.1 = f32[1,8,128,256]{3,2,1,0:T(8,128)} custom-call(f32[1,8,128,256]{3,2,1,0:T(8,128)S(1)} %source), custom_call_target="tpu_custom_call" | custom-call | tf_op jit(solution)/shard_map/cond/branch_0_fun/pallas_call | solution.py:508
Async XLA Ops:
  0.0 73.8 %copy-start = (f32[1,8,128,256]{3,2,1,0:T(8,128)S(1)}, f32[1,8,128,256]{3,2,1,0:T(8,128)}, u32[]{:S(2)}) copy-start(f32[1,8,128,256]{3,2,1,0:T(8,128)} %loads_hbm.1) | copy-start | bytes 3145732
  0.0 73.8 %copy-start.1 = (f32[512,256]{1,0:T(8,128)S(1)}, f32[512,256]{1,0:T(8,128)}, u32[]{:S(2)}) copy-start(f32[512,256]{1,0:T(8,128)} %multipliers_hbm.1) | copy-start | bytes 1572868
  0.0 73.8 %copy-start.2 = (f32[1,7,128,128]{3,2,1,0:T(8,128)S(1)}, f32[1,7,128,128]{3,2,1,0:T(8,128)}, u32[]{:S(2)}) copy-start(f32[1,7,128,128]{3,2,1,0:T(8,128)} %to_parent_hbm.1) | copy-start | bytes 1376260
  0.0 73.8 %copy-start.3 = (f32[1,6,128,128]{3,2,1,0:T(8,128)S(1)}, f32[1,6,128,128]{3,2,1,0:T(8,128)}, u32[]{:S(2)}) copy-start(f32[1,6,128,128]{3,2,1,0:T(8,128)} %grandparent_hbm.1) | copy-start | bytes 1179652
  0.0 73.8 %copy-start.4 = (s32[16,7]{0,1:T(8,128)S(1)}, s32[16,7]{0,1:T(8,128)}, u32[]{:S(2)}) copy-start(s32[16,7]{0,1:T(8,128)} %param.26) | copy-start | bytes 1348
  0.0 73.8 %copy-start.7 = (s32[512]{0:T(512)S(1)}, s32[512]{0:T(512)}, u32[]{:S(2)}) copy-start(s32[512]{0:T(512)} %param.24) | copy-start | bytes 6148
  0.0 73.8 %copy-start.8 = (s32[512]{0:T(512)S(1)}, s32[512]{0:T(512)}, u32[]{:S(2)}) copy-start(s32[512]{0:T(512)} %param.25) | copy-start | bytes 6148

commit v4 on v3

--- a/solution.py
+++ b/solution.py
@@ -5,10 +5,8 @@
 from jax.experimental.pallas import tpu as pltpu
 from jax.sharding import PartitionSpec as P
 
-CHUNKS = 4
-SLOTS = 16
-HEAD = 8
-EARLY = 2
+EARLY = 32
+LATE = 32
 
 
 def split(x):
@@ -49,12 +47,12 @@
 
     arguments = (
         (parents_hbm, parents),
+        (gluing_hbm, gluing),
+        (signs_hbm, signs),
+        (multipliers_hbm, multipliers),
         (to_parent_hbm, to_parent),
         (grandparent_hbm, grandparent),
         (inverses_hbm, inverses),
-        (gluing_hbm, gluing),
-        (signs_hbm, signs),
-        (multipliers_hbm, multipliers),
         (loads_hbm, loads),
     )
     fetches = [pltpu.make_async_copy(far, near, fetched.at[i]) for i, (far, near) in enumerate(arguments)]
@@ -68,6 +66,9 @@
         y = lax.rem(lax.div(me, 4) + shift(lax.div(k, 4)), 4)
         x = lax.rem(lax.rem(me, 4) + shift(lax.rem(k, 4)), 4)
         return 4 * y + x
+
+    apart = [(2, 2), (2, 3), (3, 2), (2, 1), (1, 2), (3, 3), (1, 1), (3, 1), (1, 3), (0, 2), (2, 0), (0, 1), (1, 0), (0, 3), (3, 0)]
+    peers = [4 * lax.rem(lax.div(me, 4) + y, 4) + lax.rem(lax.rem(me, 4) + x, 4) for y, x in apart]
 
     def copy(source, target, send, recv, device):
         return pltpu.make_async_remote_copy(
@@ -84,11 +85,8 @@
             self.source, self.target, self.send, self.recv = source, target, send, recv
 
         def start(self):
-            @pl.loop(0, others)
-            def _(k):
-                device = peer(k)
+            for device in peers:
                 copy(self.source.at[device], self.target.at[me], self.send, self.recv, device).start()
-
             self.target[me] = self.source[me]
 
         def all(self):
@@ -149,12 +147,7 @@
         hit = same & (lax.div(place_c, part) == along[:, l : l + 1])
         child_map[l] = jnp.where(hit, 1.0, 0.0).astype(jnp.bfloat16)
 
-    for fetch in fetches[1:4]:
-        fetch.wait()
-    ask(0, pair(1))
-    pl.semaphore_wait(barrier, others)
-    ask_up[0].start()
-    for fetch in fetches[4:6]:
+    for fetch in fetches[1:3]:
         fetch.wait()
 
     dof = jnp.concatenate([gluing[i : i + 1, :] for i in range(gluing.shape[0])], axis=1)
@@ -173,40 +166,40 @@
         down_key = jnp.concatenate([down_key] * (count // 128), axis=1)
         before = (down_key < key) & (down_key >= first_key)
         rank = rank + jnp.sum(jnp.where(before, 1.0, 0.0), axis=0, keepdims=True)
-    rank = rank.astype(jnp.int32)
-    fits = rank < CHUNKS * SLOTS
-    chunk = lax.div(rank, SLOTS)
-    slot = lax.rem(rank, SLOTS)
-    fine = fits & ((row >= 2 * rows) | (chunk < EARLY))
+    place = rank.astype(jnp.int32) + 1
+    fine = place < jnp.where(row < 2 * rows, EARLY, EARLY + LATE)
     overflow = jnp.max(jnp.where(fine, 0.0, 1.0))
 
-    place = jnp.where(fits, node * HEAD + chunk, -1)
-    owner_rows = lax.broadcasted_iota(jnp.int32, (nodes * HEAD, count), 0) == place
-    low_part = jnp.where(owner_rows, lax.rem(row, rows).astype(jnp.float32), 0.0).astype(jnp.bfloat16)
-    high_part = jnp.where(owner_rows, (lax.div(row, rows) * rows).astype(jnp.float32), 0.0).astype(jnp.bfloat16)
-    lane_of = lax.broadcasted_iota(jnp.int32, (nodes * SLOTS, count), 0) == SLOTS * me + slot
+    owned = lax.broadcasted_iota(jnp.int32, (nodes, count), 0) == node
+    low_part = jnp.where(owned, lax.rem(row, rows).astype(jnp.float32), 0.0).astype(jnp.bfloat16)
+    high_part = jnp.where(owned, (lax.div(row, rows) * rows).astype(jnp.float32), 0.0).astype(jnp.bfloat16)
+    lane_of = lax.broadcasted_iota(jnp.int32, (columns, count), 0) == place
     lane_of = jnp.where(lane_of, 1.0, 0.0).astype(jnp.bfloat16)
     contract = (((1,), (1,)), ((), ()))
     header = lax.dot_general(low_part, lane_of, contract, preferred_element_type=jnp.float32)
     header = header + lax.dot_general(high_part, lane_of, contract, preferred_element_type=jnp.float32)
-    last = lax.rem(lax.broadcasted_iota(jnp.int32, header.shape, 0), HEAD) == HEAD - 1
-    header = jnp.where(last, overflow, header)
-    bucket[:, 0:HEAD, :] = header.reshape(nodes, HEAD, columns)
-
-    target = jnp.where(fits, chunk * (nodes * SLOTS) + node * SLOTS + slot, -1)
-    fetches[6].wait()
+    lane = lax.broadcasted_iota(jnp.int32, header.shape, 1)
+    header = jnp.where(lane == 0, -1.0, jnp.where(lane < EARLY + LATE, header, overflow))
+
+    fetches[3].wait()
     m_high, m_low = split(multipliers[...])
 
-    def packed(j):
-        index = lax.broadcasted_iota(jnp.int32, (nodes * SLOTS, count), 0) + j * nodes * SLOTS
-        table = jnp.where(index == target, coeff, 0.0).astype(jnp.bfloat16)
-        return (mm(table, m_high) + mm(table, m_low)).reshape(nodes, SLOTS, columns)
-
-    for j in range(EARLY):
-        bucket[:, HEAD + j * SLOTS : HEAD + (j + 1) * SLOTS, :] = packed(j)
+    def packed(first, size):
+        index = lax.broadcasted_iota(jnp.int32, (nodes * size, count), 0)
+        inside = (place >= first) & (place < first + size)
+        table = jnp.where(index == jnp.where(inside, node * size + place - first, -1), coeff, 0.0).astype(jnp.bfloat16)
+        return (mm(table, m_high) + mm(table, m_low)).reshape(nodes, size, columns)
+
+    bucket[...] = packed(0, EARLY)
+    for n in range(nodes):
+        bucket[n, 0:1, :] = header[n : n + 1, :]
+    for fetch in fetches[4:7]:
+        fetch.wait()
+    ask(0, pair(1))
+    pl.semaphore_wait(barrier, others)
+    ask_up[0].start()
     pack.start()
-    for j in range(CHUNKS - EARLY):
-        late_bucket[:, j * SLOTS : (j + 1) * SLOTS, :] = packed(EARLY + j)
+    late_bucket[...] = packed(EARLY, LATE)
 
     ask(1, pair(3))
     last_step = product(halves(to_parent[0, levels - 2]), inverses[0, levels - 2])
@@ -251,35 +244,37 @@
         far[r] = halves(jnp.concatenate([leap - made[:rows], remote, step], axis=0))
 
     answer(0)
-    late_pack.start()
     ask_up[1].start()
     root_up.start()
-
-    width = nodes * SLOTS
-
-    def unpack(j, values):
-        high, low = split(values.reshape(width, columns))
-        rows_high[j * width : (j + 1) * width] = high
-        rows_low[j * width : (j + 1) * width] = low
-
-    def glue(level, chunks, wanted):
-        table = lax.broadcasted_iota(jnp.int32, (rows, chunks * width), 0) + level * rows == wanted
+    late_pack.start()
+
+    width = nodes * EARLY
+
+    def glue(level, wanted, source):
+        table = lax.broadcasted_iota(jnp.int32, (rows, wanted.shape[1]), 0) + level * rows == wanted
         table = jnp.where(table, 1.0, 0.0).astype(jnp.bfloat16)
-        glued = mm(table, rows_high[: chunks * width]) + mm(table, rows_low[: chunks * width])
-        pending[level] = loads[0, level] - glued
+        return mm(table, source[0]) + mm(table, source[1])
 
     fetches[7].wait()
     pack.arrived()
-    head = received[0, 0:HEAD, :]
-    for i in range(1, nodes):
-        head = head + received[i, 0:HEAD, :]
-    flag[0, 0] = jnp.where(jnp.max(head[HEAD - 1 :, :]) > 0.0, 1, 0)
-    wanted = jnp.concatenate([head[j : j + 1, :] for j in range(CHUNKS)], axis=1).astype(jnp.int32)
-    for j in range(EARLY):
-        unpack(j, received[:, HEAD + j * SLOTS : HEAD + (j + 1) * SLOTS, :])
-
+    head = jnp.concatenate([received[n, 0:1, :] for n in range(nodes)], axis=0)
+    flag[0, 0] = jnp.where(jnp.max(head[:, EARLY + LATE :]) > 0.0, 1, 0)
+
+    def wide(first, size):
+        lanes = lax.broadcasted_iota(jnp.int32, (columns, nodes * size), 1)
+        pick = lax.rem(lanes, size) + first == lax.broadcasted_iota(jnp.int32, (columns, nodes * size), 0)
+        pick = jnp.where(pick, 1.0, 0.0).astype(jnp.bfloat16)
+        high, low = split(head)
+        found = mm(high, pick) + mm(low, pick)
+        sender = lax.div(lax.broadcasted_iota(jnp.int32, found.shape, 1), size)
+        mine = sender == lax.broadcasted_iota(jnp.int32, found.shape, 0)
+        return jnp.sum(jnp.where(mine, found, 0.0), axis=0, keepdims=True).astype(jnp.int32)
+
+    early_rows = wide(0, EARLY)
+    high, low = split(received[...].reshape(width, columns))
+    rows_high[:width], rows_low[:width] = high, low
     for l in range(2):
-        glue(l, EARLY, wanted[:, : EARLY * width])
+        pending[l] = loads[0, l] - glue(l, early_rows, (high, low))
 
     compose(0)
 
@@ -311,12 +306,12 @@
         if r == 0:
             answer(1)
             late_pack.arrived()
-            for j in range(CHUNKS - EARLY):
-                unpack(EARLY + j, late_received[:, j * SLOTS : (j + 1) * SLOTS, :])
+            every_row = jnp.concatenate([early_rows, wide(EARLY, LATE)], axis=1)
+            rows_high[width:], rows_low[width:] = split(late_received[...].reshape(nodes * LATE, columns))
 
             @pl.loop(2, levels)
             def _(l):
-                glue(l, CHUNKS, wanted)
+                pending[l] = loads[0, l] - glue(l, every_row, (rows_high[...], rows_low[...]))
 
             root_up.arrived()
             six_in = root_in[...].reshape(rows, rows)
@@ -325,7 +320,6 @@
             item_out[4 * rounds + 1] = above.reshape(blocks)
             root_down.start()
             item_out[4 * rounds] = product(six[...], pending[levels - 2]).reshape(blocks)
-            tail_up.start()
         else:
             skipped(r - 1)
         if r == 1:
@@ -343,6 +337,8 @@
             second = gather(far_map[r, :, : 2 * rows], second)
         down_out[r, :, part:] = second.reshape(blocks)
         down[r].start()
+        if r == 1:
+            tail_up.start()
         step_up[r].arrived()
         item_out[rounds + r] = gather(parent_map[level], item_in[r].reshape(rows, columns)).reshape(blocks)
         step_down[r].start()
@@ -370,7 +366,6 @@
     _, levels, rows, columns = loads.shape
     count = multipliers.shape[0]
     f32, bf16 = jnp.float32, jnp.bfloat16
-    room = HEAD + EARLY * SLOTS
     rounds = levels // 2 - 1
     part = rows // nodes
     items = 4 * rounds + 2
@@ -394,12 +389,12 @@
             pltpu.VMEM(to_parent.shape, f32),
             pltpu.VMEM(grandparent_factor.shape, f32),
             dma((8,)),
-            pltpu.VMEM((nodes, room, columns), f32),
-            pltpu.VMEM((nodes, room, columns), f32),
-            pltpu.VMEM((nodes, (CHUNKS - EARLY) * SLOTS, columns), f32),
-            pltpu.VMEM((nodes, (CHUNKS - EARLY) * SLOTS, columns), f32),
-            pltpu.VMEM((nodes * CHUNKS * SLOTS, columns), bf16),
-            pltpu.VMEM((nodes * CHUNKS * SLOTS, columns), bf16),
+            pltpu.VMEM((nodes, EARLY, columns), f32),
+            pltpu.VMEM((nodes, EARLY, columns), f32),
+            pltpu.VMEM((nodes, LATE, columns), f32),
+            pltpu.VMEM((nodes, LATE, columns), f32),
+            pltpu.VMEM((nodes * (EARLY + LATE), columns), bf16),
+            pltpu.VMEM((nodes * (EARLY + LATE), columns), bf16),
             pltpu.VMEM((levels, rows, columns), f32),
             pltpu.VMEM((levels - 1, rows, rows), bf16),
             pltpu.VMEM((levels - 1, rows, rows), bf16),

time: 75.3 us -> 72.8 us (0.967)
  Pallas kernels: 74.1 us -> 71.6 us
    pallas_call x1, Pallas kernels: 73.1 us -> 70.5 us  [direct(): pl.pallas_call(kernel, out_shape=(jax.ShapeDtypeStruct(loads.shape, f32),...]
where the time goes in v4:
time: 72.8 us; the launch traced here: 72.7 us
  Pallas kernels  71.6 us (98%)
  between operations  0.89 us (1%)
    pallas_call x1, Pallas kernels, direct(): pl.pallas_call(kernel, out_shape=(jax.ShapeDtypeStruct(loads.shape, f32),...  70.5 us

profile of v4, /device:TPU:96, one launch (start us, length us, event | category | flops | bytes accessed | tf_op | source)
XLA Modules:
  0.0 72.7 jit_solution(11806240630656750533)
XLA Ops:
  0.0 0.0 copy-start
  0.0 0.0 copy-start.1
  0.0 0.0 copy-start.2
  0.0 0.0 copy-start.3
  0.0 0.0 copy-start.4
  0.0 0.0 copy-start.7
  0.0 0.0 copy-start.8
  0.0 70.5 %shard_map.84 = (f32[1,8,128,256]{3,2,1,0:T(8,128)S(1)}, s32[1,1]{1,0:T(1,128)}) custom-call(f32[1,8,128,256]{3,2,1,0:T(8,128)} %loads_hbm.1, f32[512,256]{1,0:T(8,128)} %multipliers_hbm.1, s32[4,128]{1,0:T(4,128)} %bitcast.82, s32[4,128]{1,0:T(4,128)} %bitcast.83, s32[7,16]{1,0:T(8,128)} %bitcast.81, f32[1,8,128,128]{3,2,1,0:T(8,128)} %inverses_hbm.1, ...), custom_call_target="tpu_custom_call" | custom-call | tf_op jit(solution)/shard_map/pallas_call | solution.py:374
  71.2 0.0 copy-done
  71.2 0.0 copy-done.1
  71.2 0.0 copy-done.2
  71.2 0.0 copy-done.3
  71.3 0.0 copy-done.4
  71.3 0.0 copy-done.7
  71.3 0.0 copy-done.8
  71.3 1.2 %conditional.1 = (f32[1,8,128,256]{3,2,1,0:T(8,128)}) conditional(s32[]{:T(128)} %bitcast.20, f32[1,8,128,256]{3,2,1,0:T(8,128)S(1)} %get-tuple-element.489, (f32[1,8,128,256]{3,2,1,0:T(8,128)S(1)}, s32[512]{0:T(512)S(1)}, f32[512,256]{1,0:T(8,128)S(1)}, s32[512]{0:T(512)S(1)}, s32[16,7]{0,1:T(8,128)S(1)}, ...), branch_computations={%region_0.0_spmd, %region_1.11_spmd} | conditional | flops 1764003968 | bytes 19699634 | solution.py:514
  71.3 1.0 %branch_0_fun.1 = f32[1,8,128,256]{3,2,1,0:T(8,128)} custom-call(f32[1,8,128,256]{3,2,1,0:T(8,128)S(1)} %source), custom_call_target="tpu_custom_call" | custom-call | tf_op jit(solution)/shard_map/cond/branch_0_fun/pallas_call | solution.py:503
Async XLA Ops:
  0.0 71.2 %copy-start = (f32[1,8,128,256]{3,2,1,0:T(8,128)S(1)}, f32[1,8,128,256]{3,2,1,0:T(8,128)}, u32[]{:S(2)}) copy-start(f32[1,8,128,256]{3,2,1,0:T(8,128)} %loads_hbm.1) | copy-start | bytes 3145732
  0.0 71.2 %copy-start.1 = (f32[512,256]{1,0:T(8,128)S(1)}, f32[512,256]{1,0:T(8,128)}, u32[]{:S(2)}) copy-start(f32[512,256]{1,0:T(8,128)} %multipliers_hbm.1) | copy-start | bytes 1572868
  0.0 71.2 %copy-start.2 = (f32[1,7,128,128]{3,2,1,0:T(8,128)S(1)}, f32[1,7,128,128]{3,2,1,0:T(8,128)}, u32[]{:S(2)}) copy-start(f32[1,7,128,128]{3,2,1,0:T(8,128)} %to_parent_hbm.1) | copy-start | bytes 1376260
  0.0 71.2 %copy-start.3 = (f32[1,6,128,128]{3,2,1,0:T(8,128)S(1)}, f32[1,6,128,128]{3,2,1,0:T(8,128)}, u32[]{:S(2)}) copy-start(f32[1,6,128,128]{3,2,1,0:T(8,128)} %grandparent_hbm.1) | copy-start | bytes 1179652
  0.0 71.2 %copy-start.4 = (s32[16,7]{0,1:T(8,128)S(1)}, s32[16,7]{0,1:T(8,128)}, u32[]{:S(2)}) copy-start(s32[16,7]{0,1:T(8,128)} %param.26) | copy-start | bytes 1348
  0.0 71.2 %copy-start.7 = (s32[512]{0:T(512)S(1)}, s32[512]{0:T(512)}, u32[]{:S(2)}) copy-start(s32[512]{0:T(512)} %param.24) | copy-start | bytes 6148
  0.0 71.2 %copy-start.8 = (s32[512]{0:T(512)S(1)}, s32[512]{0:T(512)}, u32[]{:S(2)}) copy-start(s32[512]{0:T(512)} %param.25) | copy-start | bytes 6148

commit v5 on v4

--- a/solution.py
+++ b/solution.py
@@ -7,6 +7,7 @@
 
 EARLY = 32
 LATE = 32
+PIECE = 16
 
 
 def split(x):
@@ -32,7 +33,7 @@
     out, flag,
     loads, multipliers, gluing, signs, parents, inverses, to_parent, grandparent, fetched,
     bucket, received, late_bucket, late_received, rows_high, rows_low, pending, parent_map, child_map, near_map, far_map,
-    inverse, near, far, six, step_five,
+    inverse, near, far, six, step_five, own,
     up_out, up_in, down_out, down_in, item_out, item_in, root_out, root_in,
     pack_send, pack_recv, up_send, up_recv, down_send, down_recv, item_send, item_recv, root_send, root_recv,
 ):
@@ -47,12 +48,12 @@
 
     arguments = (
         (parents_hbm, parents),
+        (to_parent_hbm, to_parent),
+        (grandparent_hbm, grandparent),
+        (inverses_hbm, inverses),
         (gluing_hbm, gluing),
         (signs_hbm, signs),
         (multipliers_hbm, multipliers),
-        (to_parent_hbm, to_parent),
-        (grandparent_hbm, grandparent),
-        (inverses_hbm, inverses),
         (loads_hbm, loads),
     )
     fetches = [pltpu.make_async_copy(far, near, fetched.at[i]) for i, (far, near) in enumerate(arguments)]
@@ -85,8 +86,11 @@
             self.source, self.target, self.send, self.recv = source, target, send, recv
 
         def start(self):
-            for device in peers:
-                copy(self.source.at[device], self.target.at[me], self.send, self.recv, device).start()
+            high = self.source.shape[1]
+            for first in range(0, high, PIECE):
+                here = pl.ds(first, min(PIECE, high))
+                for device in peers:
+                    copy(self.source.at[device, here], self.target.at[me, here], self.send, self.recv, device).start()
             self.target[me] = self.source[me]
 
         def all(self):
@@ -147,7 +151,18 @@
         hit = same & (lax.div(place_c, part) == along[:, l : l + 1])
         child_map[l] = jnp.where(hit, 1.0, 0.0).astype(jnp.bfloat16)
 
-    for fetch in fetches[1:3]:
+    for fetch in fetches[1:4]:
+        fetch.wait()
+    ask(0, pair(1))
+    ask(1, pair(3))
+    last_step = product(halves(to_parent[0, levels - 2]), inverses[0, levels - 2])
+    six[...] = halves(last_step)
+    root_out[...] = last_step.reshape(nodes, part, rows)
+    pl.semaphore_wait(barrier, others)
+    ask_up[0].start()
+    ask_up[1].start()
+    root_up.start()
+    for fetch in fetches[4:6]:
         fetch.wait()
 
     dof = jnp.concatenate([gluing[i : i + 1, :] for i in range(gluing.shape[0])], axis=1)
@@ -181,7 +196,7 @@
     lane = lax.broadcasted_iota(jnp.int32, header.shape, 1)
     header = jnp.where(lane == 0, -1.0, jnp.where(lane < EARLY + LATE, header, overflow))
 
-    fetches[3].wait()
+    fetches[6].wait()
     m_high, m_low = split(multipliers[...])
 
     def packed(first, size):
@@ -193,19 +208,10 @@
     bucket[...] = packed(0, EARLY)
     for n in range(nodes):
         bucket[n, 0:1, :] = header[n : n + 1, :]
-    for fetch in fetches[4:7]:
-        fetch.wait()
-    ask(0, pair(1))
-    pl.semaphore_wait(barrier, others)
-    ask_up[0].start()
     pack.start()
     late_bucket[...] = packed(EARLY, LATE)
 
-    ask(1, pair(3))
-    last_step = product(halves(to_parent[0, levels - 2]), inverses[0, levels - 2])
-    six[...] = halves(last_step)
-    root_out[...] = last_step.reshape(nodes, part, rows)
-    step_five[...] = pair(5)
+    own[0] = pair(0)
 
     @pl.loop(0, levels)
     def _(l):
@@ -234,8 +240,8 @@
         ask_down[r].arrived()
         found = item_in[3 * rounds + r].reshape(rows, columns)
         found = jnp.concatenate([found[:, :rows], found[:, rows:]], axis=0)
-        step = to_parent[0, 2 * r]
-        leap = grandparent[0, 2 * r]
+        step = own[r, :rows]
+        leap = own[r, rows:]
         made = product(halves(found), step)
         remote = -made[rows:]
         if r == rounds - 1:
@@ -244,8 +250,6 @@
         far[r] = halves(jnp.concatenate([leap - made[:rows], remote, step], axis=0))
 
     answer(0)
-    ask_up[1].start()
-    root_up.start()
     late_pack.start()
 
     width = nodes * EARLY
@@ -279,9 +283,7 @@
     compose(0)
 
     def solve(level, x):
-        x = product(inverse[level], x)
-        out[0, level] = x
-        return x
+        out[0, level] = product(inverse[level], x)
 
     def skipped(r):
         step_down[r].arrived()
@@ -295,15 +297,18 @@
         e = product(near[r], pending[level + 1])
         up_out[r, :, 0:part] = e[:rows].reshape(blocks)
         up_out[r, :, 2 * part : 3 * part] = e[rows:].reshape(blocks)
-        x = solve(level, pending[level])
-        c = product(far[r, : 2 * rows], x)
+        c = product(far[r, : 2 * rows], pending[level])
         up_out[r, :, part : 2 * part] = c[:rows].reshape(blocks)
         up_out[r, :, 3 * part :] = c[rows:].reshape(blocks)
         up[r].start()
-        item_out[r] = product(far[r, 2 * rows :], x).reshape(blocks)
+        item_out[r] = product(far[r, 2 * rows :], pending[level]).reshape(blocks)
         step_up[r].start()
+        solve(level, pending[level])
 
         if r == 0:
+            step_five[...] = pair(5)
+            for later in range(1, rounds):
+                own[later] = pair(2 * later)
             answer(1)
             late_pack.arrived()
             every_row = jnp.concatenate([early_rows, wide(EARLY, LATE)], axis=1)
@@ -405,6 +410,7 @@
             pltpu.VMEM((rounds, 3 * rows, 2 * rows), bf16),
             pltpu.VMEM((rows, 2 * rows), bf16),
             pltpu.VMEM((2 * rows, rows), f32),
+            pltpu.VMEM((rounds, 2 * rows, rows), f32),
             pltpu.VMEM((rounds, nodes, 4 * part, columns), f32),
             pltpu.VMEM((rounds, nodes, 4 * part, columns), f32),
             pltpu.VMEM((rounds, nodes, 2 * part, columns), f32),
@@ -511,7 +517,7 @@
 
 def body(*args):
     solved, flag = direct(*args)
-    return lax.cond(flag[0, 0] != 0, lambda: general(*args), lambda: finish(solved))
+    return lax.switch(flag[0, 0], (lambda: finish(solved), lambda: general(*args)))
 
 
 def solution(mesh):

time: 72.8 us -> 70.5 us (0.968)
  Pallas kernels: 71.6 us -> 69.3 us
    pallas_call x1, Pallas kernels: 70.5 us -> 68.3 us  [direct(): pl.pallas_call(kernel, out_shape=(jax.ShapeDtypeStruct(loads.shape, f32),...]
where the time goes in v5:
time: 70.5 us; the launch traced here: 70.4 us
  Pallas kernels  69.3 us (98%)
  between operations  0.89 us (1%)
    pallas_call x1, Pallas kernels, direct(): pl.pallas_call(kernel, out_shape=(jax.ShapeDtypeStruct(loads.shape, f32),...  68.3 us

profile of v5, /device:TPU:96, one launch (start us, length us, event | category | flops | bytes accessed | tf_op | source)
XLA Modules:
  0.0 70.4 jit_solution(13642689226290379866)
XLA Ops:
  0.0 0.0 copy-start
  0.0 0.0 copy-start.1
  0.0 0.0 copy-start.2
  0.0 0.0 copy-start.3
  0.0 0.0 copy-start.4
  0.0 0.0 copy-start.7
  0.0 0.0 copy-start.8
  0.0 68.3 %shard_map.84 = (f32[1,8,128,256]{3,2,1,0:T(8,128)S(1)}, s32[1,1]{1,0:T(1,128)}) custom-call(f32[1,8,128,256]{3,2,1,0:T(8,128)} %loads_hbm.1, f32[512,256]{1,0:T(8,128)} %multipliers_hbm.1, s32[4,128]{1,0:T(4,128)} %bitcast.82, s32[4,128]{1,0:T(4,128)} %bitcast.83, s32[7,16]{1,0:T(8,128)} %bitcast.81, f32[1,8,128,128]{3,2,1,0:T(8,128)} %inverses_hbm.1, ...), custom_call_target="tpu_custom_call" | custom-call | tf_op jit(solution)/shard_map/pallas_call | solution.py:379
  68.9 0.0 copy-done
  69.0 0.0 copy-done.1
  69.0 0.0 copy-done.2
  69.0 0.0 copy-done.3
  69.0 0.0 copy-done.4
  69.0 0.0 copy-done.7
  69.0 0.0 copy-done.8
  69.0 1.2 %conditional.1 = (f32[1,8,128,256]{3,2,1,0:T(8,128)}) conditional(s32[]{:T(128)} %bitcast.20, f32[1,8,128,256]{3,2,1,0:T(8,128)S(1)} %get-tuple-element.489, (f32[1,8,128,256]{3,2,1,0:T(8,128)S(1)}, s32[512]{0:T(512)S(1)}, f32[512,256]{1,0:T(8,128)S(1)}, s32[512]{0:T(512)S(1)}, s32[16,7]{0,1:T(8,128)S(1)}, ...), branch_computations={%region_0.0_spmd, %region_1.11_spmd} | conditional | flops 1764003968 | bytes 19699634 | solution.py:520
  69.0 1.0 %branch_0_fun.1 = f32[1,8,128,256]{3,2,1,0:T(8,128)} custom-call(f32[1,8,128,256]{3,2,1,0:T(8,128)S(1)} %source), custom_call_target="tpu_custom_call" | custom-call | tf_op jit(solution)/shard_map/cond/branch_0_fun/pallas_call | solution.py:509
Async XLA Ops:
  0.0 68.9 %copy-start = (f32[1,8,128,256]{3,2,1,0:T(8,128)S(1)}, f32[1,8,128,256]{3,2,1,0:T(8,128)}, u32[]{:S(2)}) copy-start(f32[1,8,128,256]{3,2,1,0:T(8,128)} %loads_hbm.1) | copy-start | bytes 3145732
  0.0 69.0 %copy-start.1 = (f32[512,256]{1,0:T(8,128)S(1)}, f32[512,256]{1,0:T(8,128)}, u32[]{:S(2)}) copy-start(f32[512,256]{1,0:T(8,128)} %multipliers_hbm.1) | copy-start | bytes 1572868
  0.0 69.0 %copy-start.2 = (f32[1,7,128,128]{3,2,1,0:T(8,128)S(1)}, f32[1,7,128,128]{3,2,1,0:T(8,128)}, u32[]{:S(2)}) copy-start(f32[1,7,128,128]{3,2,1,0:T(8,128)} %to_parent_hbm.1) | copy-start | bytes 1376260
  0.0 69.0 %copy-start.3 = (f32[1,6,128,128]{3,2,1,0:T(8,128)S(1)}, f32[1,6,128,128]{3,2,1,0:T(8,128)}, u32[]{:S(2)}) copy-start(f32[1,6,128,128]{3,2,1,0:T(8,128)} %grandparent_hbm.1) | copy-start | bytes 1179652
  0.0 69.0 %copy-start.4 = (s32[16,7]{0,1:T(8,128)S(1)}, s32[16,7]{0,1:T(8,128)}, u32[]{:S(2)}) copy-start(s32[16,7]{0,1:T(8,128)} %param.26) | copy-start | bytes 1348
  0.0 69.0 %copy-start.7 = (s32[512]{0:T(512)S(1)}, s32[512]{0:T(512)}, u32[]{:S(2)}) copy-start(s32[512]{0:T(512)} %param.24) | copy-start | bytes 6148
  0.0 69.0 %copy-start.8 = (s32[512]{0:T(512)S(1)}, s32[512]{0:T(512)}, u32[]{:S(2)}) copy-start(s32[512]{0:T(512)} %param.25) | copy-start | bytes 6148

commit v6 on v5

--- a/solution.py
+++ b/solution.py
@@ -86,12 +86,15 @@
             self.source, self.target, self.send, self.recv = source, target, send, recv
 
         def start(self):
-            high = self.source.shape[1]
-            for first in range(0, high, PIECE):
-                here = pl.ds(first, min(PIECE, high))
-                for device in peers:
-                    copy(self.source.at[device, here], self.target.at[me, here], self.send, self.recv, device).start()
-            self.target[me] = self.source[me]
+            for first in range(0, self.source.shape[1], PIECE):
+                self.start_piece(first)
+
+        def start_piece(self, first):
+            size = min(PIECE, self.source.shape[1])
+            here = pl.ds(first, size)
+            for device in peers:
+                copy(self.source.at[device, here], self.target.at[me, here], self.send, self.recv, device).start()
+            self.target[me, first : first + size] = self.source[me, first : first + size]
 
         def all(self):
             most = pl.ds(0, others)
@@ -109,7 +112,7 @@
     pack = Exchange(bucket, received, pack_send.at[0], pack_recv.at[0])
     late_pack = Exchange(late_bucket, late_received, pack_send.at[1], pack_recv.at[1])
     up = [Exchange(up_out.at[r], up_in.at[r], up_send.at[r], up_recv.at[r]) for r in range(rounds)]
-    down = [Exchange(down_out.at[r], down_in.at[r], down_send.at[r], down_recv.at[r]) for r in range(rounds)]
+    down = [Exchange(down_out.at[r], down_in.at[r], down_send.at[r], down_recv.at[r]) for r in range(2 * rounds)]
     step_up = [item(r) for r in range(rounds)]
     step_down = [item(rounds + r) for r in range(rounds)]
     ask_up = [item(2 * rounds + r) for r in range(rounds)]
@@ -280,8 +283,6 @@
     for l in range(2):
         pending[l] = loads[0, l] - glue(l, early_rows, (high, low))
 
-    compose(0)
-
     def solve(level, x):
         out[0, level] = product(inverse[level], x)
 
@@ -292,15 +293,21 @@
     for r in range(rounds):
         level = 2 * r
         if r > 0:
-            pending[level] = pending[level] - down_in[r - 1, :, :part].reshape(rows, columns)
-            pending[level + 1] = pending[level + 1] - down_in[r - 1, :, part:].reshape(rows, columns)
+            down[2 * r - 1].arrived()
+            pending[level + 1] = pending[level + 1] - down_in[2 * r - 1].reshape(rows, columns)
         e = product(near[r], pending[level + 1])
         up_out[r, :, 0:part] = e[:rows].reshape(blocks)
-        up_out[r, :, 2 * part : 3 * part] = e[rows:].reshape(blocks)
+        up_out[r, :, part : 2 * part] = e[rows:].reshape(blocks)
+        up[r].start_piece(0)
+        if r == 0:
+            compose(0)
+        else:
+            down[2 * r - 2].arrived()
+            pending[level] = pending[level] - down_in[2 * r - 2].reshape(rows, columns)
         c = product(far[r, : 2 * rows], pending[level])
-        up_out[r, :, part : 2 * part] = c[:rows].reshape(blocks)
+        up_out[r, :, 2 * part : 3 * part] = c[:rows].reshape(blocks)
         up_out[r, :, 3 * part :] = c[rows:].reshape(blocks)
-        up[r].start()
+        up[r].start_piece(2 * part)
         item_out[r] = product(far[r, 2 * rows :], pending[level]).reshape(blocks)
         step_up[r].start()
         solve(level, pending[level])
@@ -331,17 +338,18 @@
             answer(2)
 
         up[r].arrived()
-        first = jnp.concatenate([up_in[r, :, i * part : (i + 1) * part].reshape(rows, columns) for i in (0, 1)], axis=0)
-        down_out[r, :, :part] = gather(near_map[r], first).reshape(blocks)
-        second = jnp.concatenate([up_in[r, :, i * part : (i + 1) * part].reshape(rows, columns) for i in (2, 3)], axis=0)
+        second = jnp.concatenate([up_in[r, :, i * part : (i + 1) * part].reshape(rows, columns) for i in (1, 3)], axis=0)
         if r == rounds - 1:
             tail_up.arrived()
             second = jnp.concatenate([second, item_in[4 * rounds].reshape(rows, columns)], axis=0)
             second = gather(far_map[r], second)
         else:
             second = gather(far_map[r, :, : 2 * rows], second)
-        down_out[r, :, part:] = second.reshape(blocks)
-        down[r].start()
+        down_out[2 * r + 1] = second.reshape(blocks)
+        down[2 * r + 1].start()
+        first = jnp.concatenate([up_in[r, :, i * part : (i + 1) * part].reshape(rows, columns) for i in (0, 2)], axis=0)
+        down_out[2 * r] = gather(near_map[r], first).reshape(blocks)
+        down[2 * r].start()
         if r == 1:
             tail_up.start()
         step_up[r].arrived()
@@ -356,10 +364,11 @@
             ask_up[2].start()
         if r < rounds - 1:
             compose(r + 1)
-        down[r].arrived()
-
-    solve(levels - 2, pending[levels - 2] - down_in[rounds - 1, :, :part].reshape(rows, columns))
-    solve(levels - 1, pending[levels - 1] - down_in[rounds - 1, :, part:].reshape(rows, columns))
+
+    down[2 * rounds - 1].arrived()
+    solve(levels - 1, pending[levels - 1] - down_in[2 * rounds - 1].reshape(rows, columns))
+    down[2 * rounds - 2].arrived()
+    solve(levels - 2, pending[levels - 2] - down_in[2 * rounds - 2].reshape(rows, columns))
     skipped(rounds - 1)
 
     for exchange in everything:
@@ -413,8 +422,8 @@
             pltpu.VMEM((rounds, 2 * rows, rows), f32),
             pltpu.VMEM((rounds, nodes, 4 * part, columns), f32),
             pltpu.VMEM((rounds, nodes, 4 * part, columns), f32),
-            pltpu.VMEM((rounds, nodes, 2 * part, columns), f32),
-            pltpu.VMEM((rounds, nodes, 2 * part, columns), f32),
+            pltpu.VMEM((2 * rounds, nodes, part, columns), f32),
+            pltpu.VMEM((2 * rounds, nodes, part, columns), f32),
             pltpu.VMEM((items, nodes, part, columns), f32),
             pltpu.VMEM((items, nodes, part, columns), f32),
             pltpu.VMEM((nodes, part, rows), f32),
@@ -423,8 +432,8 @@
             dma((2,)),
             dma((rounds,)),
             dma((rounds,)),
-            dma((rounds,)),
-            dma((rounds,)),
+            dma((2 * rounds,)),
+            dma((2 * rounds,)),
             dma((items,)),
             dma((items,)),
             dma((1,)),

time: 70.5 us -> 70.2 us (level)
  no operation moved by 1% of the time
where the time goes in v6:
time: 70.2 us; the launch traced here: 70.1 us
  Pallas kernels  69 us (98%)
  between operations  0.89 us (1%)
    pallas_call x1, Pallas kernels, direct(): pl.pallas_call(kernel, out_shape=(jax.ShapeDtypeStruct(loads.shape, f32),...  68 us

profile of v6, /device:TPU:96, one launch (start us, length us, event | category | flops | bytes accessed | tf_op | source)
XLA Modules:
  0.0 70.1 jit_solution(10462325251321641823)
XLA Ops:
  0.0 0.0 copy-start
  0.0 0.0 copy-start.1
  0.0 0.0 copy-start.2
  0.0 0.0 copy-start.3
  0.0 0.0 copy-start.4
  0.0 0.0 copy-start.7
  0.0 0.0 copy-start.8
  0.0 68.0 %shard_map.84 = (f32[1,8,128,256]{3,2,1,0:T(8,128)S(1)}, s32[1,1]{1,0:T(1,128)}) custom-call(f32[1,8,128,256]{3,2,1,0:T(8,128)} %loads_hbm.1, f32[512,256]{1,0:T(8,128)} %multipliers_hbm.1, s32[4,128]{1,0:T(4,128)} %bitcast.82, s32[4,128]{1,0:T(4,128)} %bitcast.83, s32[7,16]{1,0:T(8,128)} %bitcast.81, f32[1,8,128,128]{3,2,1,0:T(8,128)} %inverses_hbm.1, ...), custom_call_target="tpu_custom_call" | custom-call | tf_op jit(solution)/shard_map/pallas_call | solution.py:388
  68.6 0.0 copy-done
  68.7 0.0 copy-done.1
  68.7 0.0 copy-done.2
  68.7 0.0 copy-done.3
  68.7 0.0 copy-done.4
  68.7 0.0 copy-done.7
  68.7 0.0 copy-done.8
  68.7 1.2 %conditional.1 = (f32[1,8,128,256]{3,2,1,0:T(8,128)}) conditional(s32[]{:T(128)} %bitcast.20, f32[1,8,128,256]{3,2,1,0:T(8,128)S(1)} %get-tuple-element.489, (f32[1,8,128,256]{3,2,1,0:T(8,128)S(1)}, s32[512]{0:T(512)S(1)}, f32[512,256]{1,0:T(8,128)S(1)}, s32[512]{0:T(512)S(1)}, s32[16,7]{0,1:T(8,128)S(1)}, ...), branch_computations={%region_0.0_spmd, %region_1.11_spmd} | conditional | flops 1764003968 | bytes 19699634 | solution.py:529
  68.7 1.0 %branch_0_fun.1 = f32[1,8,128,256]{3,2,1,0:T(8,128)} custom-call(f32[1,8,128,256]{3,2,1,0:T(8,128)S(1)} %source), custom_call_target="tpu_custom_call" | custom-call | tf_op jit(solution)/shard_map/cond/branch_0_fun/pallas_call | solution.py:518
Async XLA Ops:
  0.0 68.7 %copy-start = (f32[1,8,128,256]{3,2,1,0:T(8,128)S(1)}, f32[1,8,128,256]{3,2,1,0:T(8,128)}, u32[]{:S(2)}) copy-start(f32[1,8,128,256]{3,2,1,0:T(8,128)} %loads_hbm.1) | copy-start | bytes 3145732
  0.0 68.7 %copy-start.1 = (f32[512,256]{1,0:T(8,128)S(1)}, f32[512,256]{1,0:T(8,128)}, u32[]{:S(2)}) copy-start(f32[512,256]{1,0:T(8,128)} %multipliers_hbm.1) | copy-start | bytes 1572868
  0.0 68.7 %copy-start.2 = (f32[1,7,128,128]{3,2,1,0:T(8,128)S(1)}, f32[1,7,128,128]{3,2,1,0:T(8,128)}, u32[]{:S(2)}) copy-start(f32[1,7,128,128]{3,2,1,0:T(8,128)} %to_parent_hbm.1) | copy-start | bytes 1376260
  0.0 68.7 %copy-start.3 = (f32[1,6,128,128]{3,2,1,0:T(8,128)S(1)}, f32[1,6,128,128]{3,2,1,0:T(8,128)}, u32[]{:S(2)}) copy-start(f32[1,6,128,128]{3,2,1,0:T(8,128)} %grandparent_hbm.1) | copy-start | bytes 1179652
  0.0 68.7 %copy-start.4 = (s32[16,7]{0,1:T(8,128)S(1)}, s32[16,7]{0,1:T(8,128)}, u32[]{:S(2)}) copy-start(s32[16,7]{0,1:T(8,128)} %param.26) | copy-start | bytes 1348
  0.0 68.7 %copy-start.7 = (s32[512]{0:T(512)S(1)}, s32[512]{0:T(512)}, u32[]{:S(2)}) copy-start(s32[512]{0:T(512)} %param.24) | copy-start | bytes 6148
  0.0 68.7 %copy-start.8 = (s32[512]{0:T(512)S(1)}, s32[512]{0:T(512)}, u32[]{:S(2)}) copy-start(s32[512]{0:T(512)} %param.25) | copy-start | bytes 6148

commit v7 on v6

--- a/solution.py
+++ b/solution.py
@@ -57,17 +57,6 @@
         (loads_hbm, loads),
     )
     fetches = [pltpu.make_async_copy(far, near, fetched.at[i]) for i, (far, near) in enumerate(arguments)]
-    for fetch in fetches:
-        fetch.start()
-
-    def peer(k):
-        def shift(t):
-            return jnp.where(t < 2, t + 2, 3 - t)
-
-        y = lax.rem(lax.div(me, 4) + shift(lax.div(k, 4)), 4)
-        x = lax.rem(lax.rem(me, 4) + shift(lax.rem(k, 4)), 4)
-        return 4 * y + x
-
     apart = [(2, 2), (2, 3), (3, 2), (2, 1), (1, 2), (3, 3), (1, 1), (3, 1), (1, 3), (0, 2), (2, 0), (0, 1), (1, 0), (0, 3), (3, 0)]
     peers = [4 * lax.rem(lax.div(me, 4) + y, 4) + lax.rem(lax.rem(me, 4) + x, 4) for y, x in apart]
 
@@ -98,7 +87,7 @@
 
         def all(self):
             most = pl.ds(0, others)
-            return copy(self.source.at[most], self.target.at[most], self.send, self.recv, peer(0))
+            return copy(self.source.at[most], self.target.at[most], self.send, self.recv, peers[0])
 
         def arrived(self):
             self.all().wait_recv()
@@ -123,10 +112,10 @@
     everything = [pack, late_pack, *up, *down, *step_up, *step_down, *ask_up, *ask_down, tail_up, root_down, root_up]
 
     barrier = pltpu.get_barrier_semaphore()
-
-    @pl.loop(0, others)
-    def _(k):
-        pl.semaphore_signal(barrier, inc=1, device_id={"group": peer(k)}, device_id_type=pl.DeviceIdType.MESH)
+    for device in peers:
+        pl.semaphore_signal(barrier, inc=1, device_id={"group": device}, device_id_type=pl.DeviceIdType.MESH)
+    for fetch in fetches:
+        fetch.start()
 
     def pair(level):
         both = jnp.concatenate([to_parent[0, level], grandparent[0, level]], axis=0)

time: 70.2 us -> 70.1 us (level)
  no operation moved by 1% of the time
where the time goes in v7:
time: 70.1 us; the launch traced here: 70 us
  Pallas kernels  68.9 us (98%)
  between operations  0.89 us (1%)
    pallas_call x1, Pallas kernels, direct(): pl.pallas_call(kernel, out_shape=(jax.ShapeDtypeStruct(loads.shape, f32),...  67.9 us

profile of v7, /device:TPU:96, one launch (start us, length us, event | category | flops | bytes accessed | tf_op | source)
XLA Modules:
  0.0 70.0 jit_solution(9231138271842092074)
XLA Ops:
  0.0 0.0 copy-start
  0.0 0.0 copy-start.1
  0.0 0.0 copy-start.2
  0.0 0.0 copy-start.3
  0.0 0.0 copy-start.4
  0.0 0.0 copy-start.7
  0.0 0.0 copy-start.8
  0.0 67.9 %shard_map.84 = (f32[1,8,128,256]{3,2,1,0:T(8,128)S(1)}, s32[1,1]{1,0:T(1,128)}) custom-call(f32[1,8,128,256]{3,2,1,0:T(8,128)} %loads_hbm.1, f32[512,256]{1,0:T(8,128)} %multipliers_hbm.1, s32[4,128]{1,0:T(4,128)} %bitcast.82, s32[4,128]{1,0:T(4,128)} %bitcast.83, s32[7,16]{1,0:T(8,128)} %bitcast.81, f32[1,8,128,128]{3,2,1,0:T(8,128)} %inverses_hbm.1, ...), custom_call_target="tpu_custom_call" | custom-call | tf_op jit(solution)/shard_map/pallas_call | solution.py:377
  68.6 0.0 copy-done
  68.6 0.0 copy-done.1
  68.6 0.0 copy-done.2
  68.6 0.0 copy-done.3
  68.6 0.0 copy-done.4
  68.6 0.0 copy-done.7
  68.6 0.0 copy-done.8
  68.6 1.2 %conditional.1 = (f32[1,8,128,256]{3,2,1,0:T(8,128)}) conditional(s32[]{:T(128)} %bitcast.20, f32[1,8,128,256]{3,2,1,0:T(8,128)S(1)} %get-tuple-element.489, (f32[1,8,128,256]{3,2,1,0:T(8,128)S(1)}, s32[512]{0:T(512)S(1)}, f32[512,256]{1,0:T(8,128)S(1)}, s32[512]{0:T(512)S(1)}, s32[16,7]{0,1:T(8,128)S(1)}, ...), branch_computations={%region_0.0_spmd, %region_1.11_spmd} | conditional | flops 1764003968 | bytes 19699634 | solution.py:518
  68.6 1.0 %branch_0_fun.1 = f32[1,8,128,256]{3,2,1,0:T(8,128)} custom-call(f32[1,8,128,256]{3,2,1,0:T(8,128)S(1)} %source), custom_call_target="tpu_custom_call" | custom-call | tf_op jit(solution)/shard_map/cond/branch_0_fun/pallas_call | solution.py:507
Async XLA Ops:
  0.0 68.6 %copy-start = (f32[1,8,128,256]{3,2,1,0:T(8,128)S(1)}, f32[1,8,128,256]{3,2,1,0:T(8,128)}, u32[]{:S(2)}) copy-start(f32[1,8,128,256]{3,2,1,0:T(8,128)} %loads_hbm.1) | copy-start | bytes 3145732
  0.0 68.6 %copy-start.1 = (f32[512,256]{1,0:T(8,128)S(1)}, f32[512,256]{1,0:T(8,128)}, u32[]{:S(2)}) copy-start(f32[512,256]{1,0:T(8,128)} %multipliers_hbm.1) | copy-start | bytes 1572868
  0.0 68.6 %copy-start.2 = (f32[1,7,128,128]{3,2,1,0:T(8,128)S(1)}, f32[1,7,128,128]{3,2,1,0:T(8,128)}, u32[]{:S(2)}) copy-start(f32[1,7,128,128]{3,2,1,0:T(8,128)} %to_parent_hbm.1) | copy-start | bytes 1376260
  0.0 68.6 %copy-start.3 = (f32[1,6,128,128]{3,2,1,0:T(8,128)S(1)}, f32[1,6,128,128]{3,2,1,0:T(8,128)}, u32[]{:S(2)}) copy-start(f32[1,6,128,128]{3,2,1,0:T(8,128)} %grandparent_hbm.1) | copy-start | bytes 1179652
  0.0 68.6 %copy-start.4 = (s32[16,7]{0,1:T(8,128)S(1)}, s32[16,7]{0,1:T(8,128)}, u32[]{:S(2)}) copy-start(s32[16,7]{0,1:T(8,128)} %param.26) | copy-start | bytes 1348
  0.0 68.6 %copy-start.7 = (s32[512]{0:T(512)S(1)}, s32[512]{0:T(512)}, u32[]{:S(2)}) copy-start(s32[512]{0:T(512)} %param.24) | copy-start | bytes 6148
  0.0 68.6 %copy-start.8 = (s32[512]{0:T(512)S(1)}, s32[512]{0:T(512)}, u32[]{:S(2)}) copy-start(s32[512]{0:T(512)} %param.25) | copy-start | bytes 6148

commit v8 on v7

--- a/solution.py
+++ b/solution.py
@@ -302,10 +302,10 @@
         solve(level, pending[level])
 
         if r == 0:
+            answer(1)
             step_five[...] = pair(5)
             for later in range(1, rounds):
                 own[later] = pair(2 * later)
-            answer(1)
             late_pack.arrived()
             every_row = jnp.concatenate([early_rows, wide(EARLY, LATE)], axis=1)
             rows_high[width:], rows_low[width:] = split(late_received[...].reshape(nodes * LATE, columns))

time: 70.1 us -> 70.1 us (level)
  no operation moved by 1% of the time
where the time goes in v8:
time: 70.1 us; the launch traced here: 70 us
  Pallas kernels  68.9 us (98%)
  between operations  0.89 us (1%)
    pallas_call x1, Pallas kernels, direct(): pl.pallas_call(kernel, out_shape=(jax.ShapeDtypeStruct(loads.shape, f32),...  67.9 us

profile of v8, /device:TPU:96, one launch (start us, length us, event | category | flops | bytes accessed | tf_op | source)
XLA Modules:
  0.0 70.0 jit_solution(5352095569678920884)
XLA Ops:
  0.0 0.0 copy-start
  0.0 0.0 copy-start.1
  0.0 0.0 copy-start.2
  0.0 0.0 copy-start.3
  0.0 0.0 copy-start.4
  0.0 0.0 copy-start.7
  0.0 0.0 copy-start.8
  0.0 67.9 %shard_map.84 = (f32[1,8,128,256]{3,2,1,0:T(8,128)S(1)}, s32[1,1]{1,0:T(1,128)}) custom-call(f32[1,8,128,256]{3,2,1,0:T(8,128)} %loads_hbm.1, f32[512,256]{1,0:T(8,128)} %multipliers_hbm.1, s32[4,128]{1,0:T(4,128)} %bitcast.82, s32[4,128]{1,0:T(4,128)} %bitcast.83, s32[7,16]{1,0:T(8,128)} %bitcast.81, f32[1,8,128,128]{3,2,1,0:T(8,128)} %inverses_hbm.1, ...), custom_call_target="tpu_custom_call" | custom-call | tf_op jit(solution)/shard_map/pallas_call | solution.py:377
  68.6 0.0 copy-done
  68.6 0.0 copy-done.1
  68.6 0.0 copy-done.2
  68.6 0.0 copy-done.3
  68.6 0.0 copy-done.4
  68.6 0.0 copy-done.7
  68.6 0.0 copy-done.8
  68.6 1.2 %conditional.1 = (f32[1,8,128,256]{3,2,1,0:T(8,128)}) conditional(s32[]{:T(128)} %bitcast.20, f32[1,8,128,256]{3,2,1,0:T(8,128)S(1)} %get-tuple-element.489, (f32[1,8,128,256]{3,2,1,0:T(8,128)S(1)}, s32[512]{0:T(512)S(1)}, f32[512,256]{1,0:T(8,128)S(1)}, s32[512]{0:T(512)S(1)}, s32[16,7]{0,1:T(8,128)S(1)}, ...), branch_computations={%region_0.0_spmd, %region_1.11_spmd} | conditional | flops 1764003968 | bytes 19699634 | solution.py:518
  68.6 1.0 %branch_0_fun.1 = f32[1,8,128,256]{3,2,1,0:T(8,128)} custom-call(f32[1,8,128,256]{3,2,1,0:T(8,128)S(1)} %source), custom_call_target="tpu_custom_call" | custom-call | tf_op jit(solution)/shard_map/cond/branch_0_fun/pallas_call | solution.py:507
Async XLA Ops:
  0.0 68.6 %copy-start = (f32[1,8,128,256]{3,2,1,0:T(8,128)S(1)}, f32[1,8,128,256]{3,2,1,0:T(8,128)}, u32[]{:S(2)}) copy-start(f32[1,8,128,256]{3,2,1,0:T(8,128)} %loads_hbm.1) | copy-start | bytes 3145732
  0.0 68.6 %copy-start.1 = (f32[512,256]{1,0:T(8,128)S(1)}, f32[512,256]{1,0:T(8,128)}, u32[]{:S(2)}) copy-start(f32[512,256]{1,0:T(8,128)} %multipliers_hbm.1) | copy-start | bytes 1572868
  0.0 68.6 %copy-start.2 = (f32[1,7,128,128]{3,2,1,0:T(8,128)S(1)}, f32[1,7,128,128]{3,2,1,0:T(8,128)}, u32[]{:S(2)}) copy-start(f32[1,7,128,128]{3,2,1,0:T(8,128)} %to_parent_hbm.1) | copy-start | bytes 1376260
  0.0 68.6 %copy-start.3 = (f32[1,6,128,128]{3,2,1,0:T(8,128)S(1)}, f32[1,6,128,128]{3,2,1,0:T(8,128)}, u32[]{:S(2)}) copy-start(f32[1,6,128,128]{3,2,1,0:T(8,128)} %grandparent_hbm.1) | copy-start | bytes 1179652
  0.0 68.6 %copy-start.4 = (s32[16,7]{0,1:T(8,128)S(1)}, s32[16,7]{0,1:T(8,128)}, u32[]{:S(2)}) copy-start(s32[16,7]{0,1:T(8,128)} %param.26) | copy-start | bytes 1348
  0.0 68.6 %copy-start.7 = (s32[512]{0:T(512)S(1)}, s32[512]{0:T(512)}, u32[]{:S(2)}) copy-start(s32[512]{0:T(512)} %param.24) | copy-start | bytes 6148
  0.0 68.6 %copy-start.8 = (s32[512]{0:T(512)S(1)}, s32[512]{0:T(512)}, u32[]{:S(2)}) copy-start(s32[512]{0:T(512)} %param.25) | copy-start | bytes 6148
